TPU v7x, 32 devices: a whole 2x2x4 slice. The times are simulated.
32 devices in a mesh: dp: 4 (over y, x), mp: 8 (over z, core).
Axes of the slice: x: 2, y: 2, z: 4, core: 2. Of those that a mesh axis runs over, the one named last changes fastest.
Arguments:
- inputs: bfloat16 [3, 2048, 2, 2048], P(None, ('dp', 'mp')), may hold values from -6 to 6
- cotangent: bfloat16 [3, 2048, 2, 2048], P(None, ('dp', 'mp')), may hold values from -6 to 6
- doc_ids: int32 [3, 2, 2048], replicated, may hold values from 0 to 7, as said below
- gain_attn: float32 [2048], replicated, may hold values from 0.5 to 1.5
- w_query: bfloat16 [2048, 2048], P('dp', 'mp'), may hold values from -0.1875 to 0.1875
- w_key: bfloat16 [2048, 2048], P('dp', 'mp'), may hold values from -0.125 to 0.125
- w_value: bfloat16 [2048, 2048], P('dp', 'mp'), may hold values from -0.125 to 0.125
- w_out: bfloat16 [2048, 2048], P('mp', 'dp'), may hold values from -3 to 3
- gain_ffn: float32 [2048], replicated, may hold values from 0.5 to 1.5
- w_gate: bfloat16 [2048, 8192], P('dp', 'mp'), may hold values from -0.125 to 0.125
- w_up: bfloat16 [2048, 8192], P('dp', 'mp'), may hold values from -0.125 to 0.125
- w_down: bfloat16 [8192, 2048], P('mp', 'dp'), may hold values from -0.0625 to 0.0625
Outputs:
- outputs: bfloat16 [3, 2048, 2, 2048], P(None, ('dp', 'mp'))
- input_grad: float32 [3, 2048, 2, 2048], P(None, ('dp', 'mp'))
- grad_gain_attn: float32 [2048], replicated
- grad_query: float32 [2048, 2048], P('dp', 'mp')
- grad_key: float32 [2048, 2048], P('dp', 'mp')
- grad_value: float32 [2048, 2048], P('dp', 'mp')
- grad_out: float32 [2048, 2048], P('mp', 'dp')
- grad_gain_ffn: float32 [2048], replicated
- grad_gate: float32 [2048, 8192], P('dp', 'mp')
- grad_up: float32 [2048, 8192], P('dp', 'mp')
- grad_down: float32 [8192, 2048], P('mp', 'dp')
Inputs may be any that keep to these rules, and one draw needn't show every extreme that they name: `doc_ids`: in each sequence the numbers never fall along the tokens, start at 0 and take every value up to 7; one document begins within the first 512 tokens and ends within the last 512.
All inputs are finite; a program needn't handle non-finite values.
Results may differ from a plain program's by a relative error of at most 0.018.
Values may be sent and summed in bfloat16 or wider, within the bound.
A program may use at most 168 MiB of HBM per device.

v0:
```python
import functools
import math

import jax
import jax.numpy as jnp
import numpy as np
from jax import lax
from jax.experimental import pallas as pl
from jax.experimental.pallas import tpu as pltpu
from jax.sharding import PartitionSpec as P

HEAD = 128
epsilon = 1e-05
rope_base = 10000.0
F32 = jnp.float32
BF16 = jnp.bfloat16


def full_tables(total):
    half_size = HEAD // 2
    exponents = -(np.arange(half_size, dtype=np.float32) * np.float32(2.0 / HEAD))
    inverse = np.power(np.float32(rope_base), exponents)
    angles = np.arange(total, dtype=np.float32)[:, None] * inverse[None, :]
    cosine, sine = np.cos(angles), np.sin(angles)
    return (
        jnp.asarray(np.concatenate([cosine, cosine], axis=-1)),
        jnp.asarray(np.concatenate([-sine, sine], axis=-1)),
    )


def swap_halves(values):
    half_size = HEAD // 2
    return jnp.concatenate([values[..., half_size:], values[..., :half_size]], axis=-1)


def dot(left, right):
    return jnp.dot(left, right, preferred_element_type=F32)


def dot_tn(left, right):
    return lax.dot_general(left, right, (((0,), (0,)), ((), ())), preferred_element_type=F32)


def dot_nt(left, right):
    return lax.dot_general(left, right, (((1,), (1,)), ((), ())), preferred_element_type=F32)


def norm_factor(values):
    return lax.rsqrt(jnp.mean(values * values, axis=-1, keepdims=True) + epsilon)


def norm_back(values, factor, gain, incoming):
    scaled = incoming * gain
    gain_term = jnp.sum(incoming * values * factor, axis=0)
    input_term = factor * scaled - values * factor**3 * jnp.mean(
        scaled * values, axis=-1, keepdims=True
    )
    return (input_term, gain_term)


def sigmoid_of(raw, scale, shift):
    return 1.0 / (1.0 + jnp.exp(shift - raw * scale))


def split_cores(core, values, rows_here):
    shaped = values.reshape(-1, 2, rows_here, values.shape[-1])
    first, second = shaped[:, 0], shaped[:, 1]
    is_first = core == 0
    return jnp.where(is_first, first, second), jnp.where(is_first, second, first)

MESH = pl.DeviceIdType.MESH


class Spot:
    def __init__(self):
        self.dp, self.mp = lax.axis_index("dp"), lax.axis_index("mp")
        self.dp_size, self.mp_size = lax.axis_size("dp"), lax.axis_size("mp")
        self.places = self.mp_size // 2
        self.place, self.core = lax.div(self.mp, 2), lax.rem(self.mp, 2)
        self.sibling = (self.dp, self.mp + 1 - 2 * self.core)
        self.right = (self.dp, self.mp + 2)
        self.left = (self.dp, self.mp - 2)
        self.has_right = self.place < self.places - 1
        self.has_left = self.place > 0

    def peer(self, step):
        return lax.rem(self.dp + step, self.dp_size)

    def enter(self, with_dp, with_mp):
        barrier = pltpu.get_barrier_semaphore()
        count = 0

        def greet(device):
            pl.semaphore_signal(barrier, inc=1, device_id=device, device_id_type=MESH)

        if with_mp:
            greet(self.sibling)
            pl.when(self.has_right)(lambda: greet(self.right))
            pl.when(self.has_left)(lambda: greet(self.left))
            count += 1 + self.has_right.astype(jnp.int32) + self.has_left.astype(jnp.int32)
        if with_dp:
            for step in range(1, self.dp_size):
                greet((self.peer(step), self.mp))
            count += self.dp_size - 1
        pl.semaphore_wait(barrier, count)


class Swap:
    def __init__(self, spot, source, target, send, receive):
        self.spot, self.source, self.target = spot, source, target
        self.send, self.receive = send, receive
        self.copies = [self.copy(step) for step in range(1, spot.dp_size)]

    def copy(self, step):
        spot = self.spot
        return pltpu.make_async_remote_copy(
            src_ref=self.source.at[spot.peer(step)],
            dst_ref=self.target.at[spot.dp],
            send_sem=self.send.at[step],
            recv_sem=self.receive.at[step],
            device_id=(spot.peer(step), spot.mp),
            device_id_type=MESH,
        )

    def start(self):
        for copy in self.copies:
            copy.start()
        self.keep()

    def keep(self):
        self.target[self.spot.dp] = self.source[self.spot.dp]

    def wait(self):
        for copy in self.copies:
            copy.wait()


class Gather:
    def __init__(self, spot, shard, window, sems):
        self.local = pltpu.make_async_copy(shard, window(spot.dp), sems.at[0, 0])
        self.copies = [
            pltpu.make_async_remote_copy(
                src_ref=shard,
                dst_ref=window(spot.dp),
                send_sem=sems.at[0, step],
                recv_sem=sems.at[1, step],
                device_id=(spot.peer(step), spot.mp),
                device_id_type=MESH,
            )
            for step in range(1, spot.dp_size)
        ]

    def start(self):
        for copy in self.copies:
            copy.start()
        self.local.start()

    def go_on(self):
        pass

    def wait(self):
        for copy in self.copies:
            copy.wait()
        self.local.wait()


def gather_of(spot, *arguments):
    return (RingGather if spot.dp_size == 4 else Gather)(spot, *arguments)


class RingGather:
    def __init__(self, spot, shard, window, sems):
        side = spot.dp + 1 - 2 * lax.rem(spot.dp, 2)
        across = spot.dp + 2 - 4 * lax.div(spot.dp, 2)

        def copy(source, index, kind, to, half=None):
            return pltpu.make_async_remote_copy(
                src_ref=source,
                dst_ref=window(index, half),
                send_sem=sems.at[0, kind],
                recv_sem=sems.at[1, kind],
                device_id=(to, spot.mp),
                device_id_type=MESH,
            )

        self.local = pltpu.make_async_copy(shard, window(spot.dp), sems.at[0, 4])
        self.to_side = copy(shard, spot.dp, 0, side)
        self.to_across = copy(shard, spot.dp, 1, across)
        self.on_across = copy(window(side, 0), side, 2, across, 0)
        self.on_side = copy(window(across, 1), across, 3, side, 1)

    def start(self):
        self.to_side.start()
        self.to_across.start()
        self.local.start()

    def go_on(self):
        self.to_side.wait_recv()
        self.on_across.start()
        self.to_across.wait_recv()
        self.on_side.start()

    def wait(self):
        self.to_side.wait_send()
        self.to_across.wait_send()
        self.on_across.wait()
        self.on_side.wait()
        self.local.wait()


class Spread:
    def __init__(self, spot, shard, full, sems):
        self.spot, self.shard, self.full, self.sems = spot, shard, full, sems
        self.local = pltpu.make_async_copy(shard, full.at[spot.mp], sems.at[6, 0])

    def copy(self, kind, device, p, source=None, core=None):
        at = 2 * p + (self.spot.core if core is None else core)
        return pltpu.make_async_remote_copy(
            src_ref=self.full.at[at] if source is None else source,
            dst_ref=self.full.at[at],
            send_sem=self.sems.at[kind, p],
            recv_sem=self.sems.at[kind + 1, p],
            device_id=device,
            device_id_type=MESH,
        )

    def rightward(self, p, source=None):
        return self.copy(0, self.spot.right, p, source)

    def leftward(self, p, source=None):
        return self.copy(2, self.spot.left, p, source)

    def across(self, p, source=None):
        return self.copy(4, self.spot.sibling, p, source)

    def begin(self):
        spot = self.spot
        pl.when(spot.has_right)(lambda: self.rightward(spot.place, self.shard).start())
        pl.when(spot.has_left)(lambda: self.leftward(spot.place, self.shard).start())
        self.across(spot.place, self.shard).start()
        self.local.start()

    def go_on(self, hop):
        spot = self.spot

        @pl.when(spot.place >= hop)
        def _():
            p = spot.place - hop
            self.rightward(p).wait_recv()
            pl.when(spot.has_right)(lambda: self.rightward(p).start())
            self.across(p).start()

        @pl.when(spot.place + hop < spot.places)
        def _():
            p = spot.place + hop
            self.leftward(p).wait_recv()
            pl.when(spot.has_left)(lambda: self.leftward(p).start())
            self.across(p).start()

    def finish(self):
        spot = self.spot
        for p in range(spot.places):
            self.copy(4, spot.sibling, p, core=1 - spot.core).wait_recv()
            self.across(p).wait_send()
            pl.when(spot.has_right & (spot.place >= p))(lambda: self.rightward(p).wait_send())
            pl.when(spot.has_left & (spot.place <= p))(lambda: self.leftward(p).wait_send())
        self.local.wait()


def spread_scratch(places):
    return [pltpu.SemaphoreType.DMA((7, places))]


class Ship(Swap):
    def __init__(self, spot, source, target, sems):
        super().__init__(spot, source, target, sems.at[0], sems.at[1])
        self.local = pltpu.make_async_copy(source.at[spot.dp], target.at[spot.dp], sems.at[0, 0])

    def start(self):
        for copy in self.copies:
            copy.start()
        self.local.start()

    def wait(self):
        super().wait()
        self.local.wait()


def window_of(full, axis, step, column=0, columns=None):
    def window(index, half=None):
        rows = step if axis == 0 else full.shape[0]
        first, count = (0, rows) if half is None else (half * (rows // 2), rows // 2)
        if axis == 1:
            return full.at[
                pl.ds(first, count), pl.ds(pl.multiple_of(index * step, step), step)
            ]
        along = pl.ds(pl.multiple_of(index * step + first, count), count)
        return full.at[along, pl.ds(column, full.shape[1] if columns is None else columns)]

    return window


def swap_scratch(size, *block):
    return [
        pltpu.VMEM((size, *block), BF16),
        pltpu.VMEM((size, *block), BF16),
        pltpu.SemaphoreType.DMA((size,)),
        pltpu.SemaphoreType.DMA((size,)),
    ]


def far_first(places):
    orders = []
    for place in range(places):
        right, left, order = list(range(places - 1, place, -1)), list(range(place)), []
        while right or left:
            order += right[:1] + left[:1]
            right, left = right[1:], left[1:]
        orders.append(order + [place])
    return orders


class Sum:
    def __init__(self, spot, mine, out, from_sibling, passed, sems):
        self.spot = spot
        self.mine, self.out = mine, out
        self.from_sibling, self.passed = from_sibling, passed
        self.sems = sems
        self.orders = far_first(spot.places)

    def copy(self, source, target, kind, t, device, to=None):
        return pltpu.make_async_remote_copy(
            src_ref=source.at[t],
            dst_ref=target.at[t if to is None else to],
            send_sem=self.sems.at[kind, t],
            recv_sem=self.sems.at[kind + 1, t],
            device_id=device,
            device_id_type=MESH,
        )

    def sibling(self, t):
        return self.copy(self.out, self.from_sibling, 0, t, self.spot.sibling)

    def rightward(self, t):
        return self.copy(self.mine, self.passed, 2, t, self.spot.right)

    def leftward(self, t, place):
        to = jnp.where(t == place, self.spot.places, t)
        return self.copy(self.mine, self.passed, 4, t, self.spot.left, to)

    def leftward_out(self, t):
        return self.leftward(t, self.spot.place - 1)

    def leftward_in(self, t):
        return self.leftward(t, self.spot.place)

    def term(self, s):
        chosen = 0
        for place, order in enumerate(self.orders):
            for at, t in enumerate(order):
                if t:
                    chosen = chosen + jnp.where((self.spot.place == place) & (s == at), t, 0)
        return chosen

    def add(self, t, arrived):
        self.mine[t] = (self.mine[t].astype(F32) + arrived.astype(F32)).astype(BF16)

    def absorb(self, t):
        self.sibling(t).wait_recv()
        self.add(t, self.from_sibling[t])

    def begin(self, s):
        spot = self.spot

        @pl.when((spot.place == 0) & (s < spot.places - 1))
        def _():
            t = spot.places - 1 - s
            self.absorb(t)
            self.rightward(t).start()

        @pl.when((spot.place == spot.places - 1) & (s < spot.places - 1))
        def _():
            self.absorb(s)
            self.leftward_out(s).start()

    def go_on(self, hop):
        spot = self.spot
        last = spot.places - 1

        @pl.when((spot.place > 0) & (spot.place <= hop))
        def _():
            t = last + spot.place - hop
            self.absorb(t)
            self.rightward(t).wait_recv()
            self.add(t, self.passed[t])
            self.rightward(t).start()

        @pl.when((spot.place < last) & (last - spot.place <= hop))
        def _():
            t = hop - last + spot.place
            self.absorb(t)
            self.leftward_in(t).wait_recv()
            self.add(t, self.passed[t])
            self.leftward_out(t).start()

    def finish(self):
        spot = self.spot
        t = spot.place
        self.absorb(t)

        @pl.when(spot.has_left)
        def _():
            self.rightward(t).wait_recv()
            self.add(t, self.passed[t])

        @pl.when(spot.has_right)
        def _():
            self.leftward_in(t).wait_recv()
            self.add(t, self.passed[spot.places])

        for t in range(spot.places):
            self.sibling(t).wait_send()
            pl.when(spot.place < t)(lambda: self.rightward(t).wait_send())
            pl.when(spot.place > t)(lambda: self.leftward_out(t).wait_send())
        return self.mine[spot.place].astype(F32)


def sum_scratch(places, rows_here, width):
    return [
        *[pltpu.VMEM((places, rows_here, width), BF16)] * 3,
        pltpu.VMEM((places + 1, rows_here, width), BF16),
        pltpu.SemaphoreType.DMA((6, places)),
    ]


def as_column(row):
    return jnp.broadcast_to(row, (HEAD, row.shape[1])).T[:, 0:1]


def attend_blocks(qkv, ids_ref, out, scale, shift):
    count, block = out.shape[:2]
    row_at = lax.broadcasted_iota(jnp.int32, (block, block), 0)
    col_at = lax.broadcasted_iota(jnp.int32, (block, block), 1)

    @pl.loop(0, count)
    def _(i):
        queries = qkv[i, :, 0:HEAD]
        ids = as_column(ids_ref[i])

        def add_block(j, acc, diagonal=False):
            sig = sigmoid_of(dot_nt(queries, qkv[j, :, HEAD : 2 * HEAD]), scale, shift)
            visible = ids == ids_ref[j]
            if diagonal:
                visible = visible & (col_at <= row_at)
            weights = jnp.where(visible, sig, 0.0).astype(BF16)
            return acc + dot(weights, qkv[j, :, 2 * HEAD :])

        acc = add_block(i, jnp.zeros((block, HEAD), F32), True)
        out[i] = lax.fori_loop(0, i, add_block, acc).astype(BF16)


def attend_back_blocks(
    spot, qkv, grad, ids_ref, cos_ref, sin_ref, out_q, out_kv, dq, made, midway, scale, shift
):
    count, block = grad.shape[:2]
    col_at = lax.broadcasted_iota(jnp.int32, (block, block), 0)
    row_at = lax.broadcasted_iota(jnp.int32, (block, block), 1)
    dq[...] = jnp.zeros_like(dq)

    def unrotate(values, i):
        rows = pl.ds(pl.multiple_of(i * block, block), block)
        swapped = pltpu.roll(values, HEAD // 2, 1)
        return (values * cos_ref[rows, :] - swapped * sin_ref[rows, :]).astype(BF16)

    @pl.loop(0, count)
    def _(at):
        j = spot.peer(at + 1)
        keys = qkv[j, :, HEAD : 2 * HEAD]
        values = qkv[j, :, 2 * HEAD :]
        keys_t = keys.T
        ids = as_column(ids_ref[j])

        def add_block(i, sums, diagonal=False):
            dk, dv = sums
            queries, grads = qkv[i, :, 0:HEAD], grad[i]
            sig = sigmoid_of(dot_nt(keys, queries), scale, shift)
            visible = ids == ids_ref[i]
            if diagonal:
                visible = visible & (col_at <= row_at)
            sig = jnp.where(visible, sig, 0.0)
            prob_grad = dot_nt(values, grads)
            score_grad = (prob_grad * sig * (1.0 - sig)).astype(BF16)
            dq[i] += dot(keys_t, score_grad)
            return dk + dot(score_grad, queries), dv + dot(sig.astype(BF16), grads)

        zero = jnp.zeros((block, HEAD), F32)
        dk, dv = lax.fori_loop(j + 1, count, add_block, add_block(j, (zero, zero), True))
        out_kv[j, :, 0:HEAD] = unrotate(dk * scale, j)
        out_kv[j, :, HEAD:] = dv.astype(BF16)
        pl.when(at < count - 1)(lambda: made(at + 1))
        pl.when(at == 1)(midway)

    @pl.loop(0, count)
    def _(i):
        out_q[i] = unrotate(dq[i].T * scale, i)


def take(refs, count):
    return refs[:count], refs[count:]


class Loads:
    def __init__(self, pairs, sems):
        self.copies = [
            pltpu.make_async_copy(source, target, sems.at[i])
            for i, (source, target) in enumerate(pairs)
        ]
        for copy in self.copies:
            copy.start()

    def wait(self, *which):
        for i in which or range(len(self.copies)):
            self.copies[i].wait()


def lazy_scratch(*arrays):
    return [pltpu.VMEM(array.shape, array.dtype) for array in arrays] + [
        pltpu.SemaphoreType.DMA((len(arrays),))
    ]


def put_norm(x_ref, gain_ref, out_ref):
    x = x_ref[...].astype(F32)
    out_ref[...] = (x * norm_factor(x) * gain_ref[...]).astype(BF16)


def begin_kernel(
    x_ref, gain_ref, query, key, value, out, qkv_full, out_full, first_full,
    normed, sems, spread_sems,
):
    spot = Spot()
    spot.enter(True, True)
    rows, columns = query.shape
    jobs = [
        (shard, window_of(qkv_full, 0, rows, i * columns, columns))
        for i, shard in enumerate((query, key, value))
    ]
    jobs.append((out, window_of(out_full, 1, out.shape[1])))
    gathers = [
        gather_of(spot, shard, window, sems.at[i]) for i, (shard, window) in enumerate(jobs)
    ]
    for gather in gathers:
        gather.start()
    put_norm(x_ref, gain_ref, normed)
    spread = Spread(spot, normed, first_full, spread_sems)
    spread.begin()
    spread.go_on(1)
    for gather in gathers:
        gather.go_on()
    for hop in range(2, spot.places):
        spread.go_on(hop)
    for gather in gathers:
        gather.wait()
    spread.finish()


def forward_kernel(tail, head, norms, spreads, gather_axis, heads, toks, scale, shift, *refs):
    gathers = gather_axis is not None
    tail_in, refs = take(refs, 4 * tail)
    head_in, refs = take(refs, 5 * head)
    norm_in, refs = take(refs, 2 * norms)
    spread_in, refs = take(refs, spreads - norms)
    gather_in, refs = take(refs, gathers)
    tail_out, refs = take(refs, 3 * tail)
    head_out, refs = take(refs, 2 * head)
    spread_out, refs = take(refs, spreads)
    gather_out, refs = take(refs, gathers)
    sum_refs, refs = take(refs, 5 * tail)
    head_refs, refs = take(refs, 9 * head)
    normed, refs = take(refs, norms)
    lazy, refs = take(refs, 3 * head)
    if head:
        rows_ref, weight_ref, cos_ref, sin_ref, ids_ref = head_in
        loads = Loads(zip((rows_ref, weight_ref), lazy), lazy[2])
        rows_ref, weight_ref = lazy[:2]
    spot = Spot()
    spot.enter(head or gathers, tail or spreads)
    if norms:
        put_norm(*norm_in, *normed)
        spread_in = (*normed, *spread_in)
    moving = [Spread(spot, *refs) for refs in zip(spread_in, spread_out, refs)]
    for spread in moving:
        spread.begin()
    if gathers:
        window = window_of(gather_out[0], gather_axis, gather_in[0].shape[gather_axis])
        gather = gather_of(spot, gather_in[0], window, refs[-1])
        if not (tail and head):
            gather.start()

    if tail:
        got, out_weight, x_ref, gain_ref = tail_in
        middle_ref, normed_ref, mix_ref = tail_out
        pairs = got.shape[0]
        owner_rows = toks * (pairs // heads)
        for o in range(mix_ref.shape[0] // owner_rows):
            for p in range(pairs):
                s, h = p // heads, p % heads
                mix_ref[pl.ds(o * owner_rows + s * toks, toks), h * HEAD : (h + 1) * HEAD] = got[
                    p, pl.ds(o * toks, toks), :
                ]
        summed = Sum(spot, *sum_refs)
        chip_rows = 2 * owner_rows

        @pl.loop(0, spot.places)
        def _(s):
            t = summed.term(s)
            rows = pl.ds(pl.multiple_of(t * chip_rows, chip_rows), chip_rows)
            value = dot(mix_ref[rows, :], out_weight[...]).astype(BF16)
            keep, send = split_cores(spot.core, value, owner_rows)
            summed.mine[t] = keep[0]
            summed.out[t] = send[0]
            summed.sibling(t).start()

        @pl.loop(0, spot.places - 1)
        def _(s):
            summed.begin(s)

    if head:
        qkv_ref, got_ref = head_out
        made, paired, qkv, qkv_send, qkv_recv, part, got, part_send, part_recv = head_refs
        pairs = paired.shape[0]
        owner_rows = toks * (pairs // heads)
        step = made.shape[0]
        loads.wait()

        @pl.loop(0, rows_ref.shape[0] // step)
        def _(i):
            rows = pl.ds(pl.multiple_of(i * step, step), step)
            made[...] = dot(rows_ref[rows, :], weight_ref[...])
            for j in range(step // owner_rows):
                to = pl.ds(pl.multiple_of((i * (step // owner_rows) + j) * toks, toks), toks)
                cosine, sine = cos_ref[to, :], sin_ref[to, :]
                for p in range(pairs):
                    s, h = p // heads, p % heads
                    here = pl.ds(j * owner_rows + s * toks, toks)
                    for kind in range(3):
                        piece = made[here, pl.ds((kind * heads + h) * HEAD, HEAD)]
                        if kind < 2:
                            piece = piece * cosine + pltpu.roll(piece, HEAD // 2, 1) * sine
                        paired[p, to, kind * HEAD : (kind + 1) * HEAD] = piece.astype(BF16)

        swap = Swap(spot, paired, qkv, qkv_send, qkv_recv)
        swap.start()
    if gathers and tail and head:
        gather.start()
    for spread in moving:
        spread.go_on(1)
    if tail and spot.places > 2:
        summed.go_on(1)
    if head:
        swap.wait()
        attend_blocks(qkv, ids_ref, part, scale, shift)
        swap = Swap(spot, part, got, part_send, part_recv)
        swap.start()
    for hop in range(2, spot.places - 1):
        for spread in moving:
            spread.go_on(hop)
        if tail:
            summed.go_on(hop)
    if gathers:
        gather.go_on()
    if head:
        qkv_ref[...] = qkv[...]
        swap.wait()
        got_ref[...] = got[...]
    for spread in moving:
        if spot.places > 2:
            spread.go_on(spot.places - 1)
    if tail:
        middle = x_ref[...].astype(F32) + summed.finish()
        middle_ref[...] = middle
        normed_ref[...] = (middle * norm_factor(middle) * gain_ref[...]).astype(BF16)
    for spread in moving:
        spread.finish()
    if gathers:
        gather.wait()


def middle_kernel(
    first, defer, ships, spreads, owner_rows,
    middle_ref, local_cot_ref, gain_ref, rows_in, cot_in, gate_in, up_low, up_high, down_in,
    *refs,
):
    shards, refs = take(refs, spreads)
    before, refs = take(refs, 0 if first else 3)
    (grad_ref, low_ref, gain_grad_ref), refs = take(refs, 3)
    y_out, refs = take(refs, 2 if defer else 1)
    fulls, refs = take(refs, spreads)
    after, refs = take(refs, 3)
    ship_out, refs = take(refs, ships)
    (act_ref, dgate_ref, dup_ref, turned, new_rows, new_cols, old_rows, old_cols), refs = take(refs, 8)
    (rows_ref, cot_ref, gate_ref, up_ref, down_ref, load_sems, wide_sems), refs = take(refs, 7)
    sum_refs, refs = take(refs, 5)
    y_refs, refs = take(refs, 3 if defer else 5)
    ship_sems, refs = take(refs, ships)
    size, half = after[0].shape[0], up_low.shape[0] // after[0].shape[0]
    pairs = [(rows_in, rows_ref), (gate_in, gate_ref)]
    for e in range(size):
        for i, part in enumerate((up_low, up_high)):
            to = up_ref.at[pl.ds((2 * e + i) * half, half), :]
            pairs.append((part.at[pl.ds(e * half, half), :], to))
    pairs += [(cot_in, cot_ref), (down_in, down_ref)]
    loads = Loads(pairs, load_sems)
    spot = Spot()
    spot.enter(bool(ships), True)
    if ships:
        ship = Ship(spot, after[0], ship_out[0], ship_sems[0])
    summed = Sum(spot, *sum_refs)
    if defer:
        y_mine, y_send, y_sems = y_refs
        stores = [
            pltpu.make_async_copy(source, target, y_sems.at[i])
            for i, (source, target) in enumerate(zip((y_mine, y_send), y_out))
        ]
        sums = [summed]
    else:
        summed_y = Sum(spot, *y_refs)
        y_mine, y_send = summed_y.mine, summed_y.out
        sums = [summed, summed_y]
    moving = [Spread(spot, *refs) for refs in zip(shards, fulls, refs)]
    for spread in moving:
        spread.begin()
    hidden, width = gate_ref.shape[1], rows_ref.shape[1]
    chip_rows = 2 * owner_rows
    tile = min(256, hidden)
    blocks = after[0].shape[0]
    block = width // blocks
    new = (new_rows.at[0], new_rows.at[1], new_cols)
    old = (old_rows.at[0], old_rows.at[1], old_cols)

    def load(g, e):
        return pltpu.make_async_copy(before[g].at[e], old[g], wide_sems.at[0, g])

    def store(g, e):
        return pltpu.make_async_copy(new[g], after[g].at[e], wide_sems.at[1, g])

    if not first:
        for g in range(3):
            load(g, spot.peer(1)).start()
    loads.wait()

    @pl.loop(0, spot.places)
    def _(s):
        place = summed.term(s)
        rows = pl.ds(pl.multiple_of(place * chip_rows, chip_rows), chip_rows)

        @pl.loop(0, hidden // tile)
        def _(t):
            cols = pl.ds(pl.multiple_of(t * tile, tile), tile)
            gate = dot(rows_ref[rows, :], gate_ref[:, cols])
            up = dot(rows_ref[rows, :], up_ref[:, cols])
            sig = jax.nn.sigmoid(gate)
            silu = gate * sig
            act_ref[rows, cols] = (silu * up).astype(BF16)
            grad = dot_nt(cot_ref[rows, :], down_ref[cols, :])
            dgate_ref[rows, cols] = (grad * up * sig * (1.0 + gate * (1.0 - sig))).astype(BF16)
            dup_ref[rows, cols] = (grad * silu).astype(BF16)

            @pl.when((s > 0) & (t == min(1, hidden // tile - 1)))
            def _():
                for each in sums:
                    each.begin(s - 1)

        for hop in range(1, spot.places - 1):

            @pl.when(s == hop + 1)
            def _():
                for spread in moving:
                    spread.go_on(hop)
                for each in sums:
                    each.go_on(hop)

        @pl.loop(0, width // 256)
        def _(t):
            cols = pl.ds(pl.multiple_of(t * 256, 256), 256)
            value = dot(act_ref[rows, :], down_ref[:, cols])
            keep, send = split_cores(spot.core, value.astype(BF16), owner_rows)
            y_mine[place, :, cols] = keep[0]
            y_send[place, :, cols] = send[0]
            value = dot_nt(dgate_ref[rows, :], gate_ref[cols, :])
            value += dot_nt(dup_ref[rows, :], up_ref[cols, :])
            keep, send = split_cores(spot.core, value.astype(BF16), owner_rows)
            summed.mine[place, :, cols] = keep[0]
            summed.out[place, :, cols] = send[0]

        for each in sums:
            each.sibling(place).start()

    if defer:
        for copy in stores:
            copy.start()

    def send(i):
        if ships:
            pl.when(i < blocks - 1)(lambda: ship.copy(i + 1).start())
            pl.when(i == blocks - 1)(lambda: ship.local.start())

    def make(g, i, left, right, right_at, columns):
        e = spot.peer(i + 1)

        @pl.when(i > 0)
        def _():
            store(g, spot.peer(i)).wait()
            if g == 0:
                send(i - 1)

        if not first:
            load(g, e).wait()
        step = math.gcd(columns, 256)

        @pl.loop(0, columns // step)
        def _(t):
            cols = pl.ds(pl.multiple_of(t * step, step), step)
            total = dot(left[...], right[:, pl.ds(pl.multiple_of(right_at + t * step, step), step)])
            if not first:
                total += old[g][:, cols].astype(F32)
            new[g][:, cols] = total.astype(BF16)

        if not first:
            pl.when(i < blocks - 1)(lambda: load(g, spot.peer(i + 2)).start())
        store(g, e).start()

    @pl.loop(0, blocks)
    def _(i):
        left = turned.at[pl.ds(0, block), :]
        at = spot.peer(i + 1) * block
        left[...] = rows_ref[:, pl.ds(pl.multiple_of(at, block), block)].T
        make(0, i, left, dgate_ref, 0, hidden)
        make(1, i, left, dup_ref, 0, hidden)

    if ships:
        store(0, spot.dp).wait()
        send(blocks - 1)
    for spread in moving:
        spread.go_on(spot.places - 1)
    left = turned.at[pl.ds(0, hidden), :]
    left[...] = act_ref[...].T

    @pl.loop(0, blocks)
    def _(i):
        make(2, i, left, cot_ref, spot.peer(i + 1) * block, block)

    incoming = summed.finish()
    middle = middle_ref[...]
    term, gain_grad = norm_back(middle, norm_factor(middle), gain_ref[...], incoming)
    gain_grad_ref[...] = gain_grad[None]
    grad = local_cot_ref[...].astype(F32) + term
    grad_ref[...] = grad
    low_ref[...] = grad.astype(BF16)
    if defer:
        for copy in stores:
            copy.wait()
    else:
        y_out[0][...] = (middle + summed_y.finish()).astype(BF16)
    for spread in moving:
        spread.finish()
    for g in range(ships, 3):
        store(g, spot.dp).wait()
    if ships:
        ship.wait()


def add_grads(spot, left, right, turned, before, after, made=None):
    size, rows, columns = after.shape

    @pl.loop(0, size)
    def _(i):
        e = spot.peer(i + 1)
        if rows < left.shape[1]:
            turned[...] = left[:, pl.ds(pl.multiple_of(e * rows, rows), rows)].T
            total = dot(turned[...], right[...])
        else:

            @pl.when(i == 0)
            def _():
                turned[...] = left[...].T

            cut = pl.ds(pl.multiple_of(e * columns, columns), columns)
            total = dot(turned[...], right[:, cut])
        if before is not None:
            total += before[e].astype(F32)
        after[e] = total.astype(BF16)
        if made is not None:
            made(i)


def backward_kernel(
    tail, head, last, old_tail, old_head, extra, spreads, heads, toks, scale, shift, *refs
):
    tail_in, refs = take(refs, 6 * tail)
    old_qkv, refs = take(refs, old_tail)
    head_in, refs = take(refs, 7 * head)
    old_out, refs = take(refs, old_head)
    last_in, refs = take(refs, 2 * last)
    extra_in, refs = take(refs, 3 * extra)
    spread_in, refs = take(refs, spreads)
    tail_out, refs = take(refs, (1 if last else 3) * tail)
    head_out, refs = take(refs, 2 * head)
    last_out, refs = take(refs, 3 * last)
    extra_out, refs = take(refs, extra)
    spread_out, refs = take(refs, spreads)
    tail_refs, refs = take(refs, 7 * tail)
    head_refs, refs = take(refs, 14 * head)
    last_refs, refs = take(refs, 8 * last)
    extra_refs, refs = take(refs, 6 * extra)
    lazy_tail, refs = take(refs, 3 * tail)
    lazy_old, refs = take(refs, 2 * old_tail)
    lazy_head, refs = take(refs, 5 * head)
    if head:
        rows_ref, out_weight_ref, qkv, ids_ref, cos_ref, sin_ref, mix_ref = head_in
        loads_head = Loads(zip((rows_ref, qkv, cos_ref, sin_ref), lazy_head), lazy_head[4])
        rows_ref, qkv, cos_ref, sin_ref = lazy_head[:4]
    if tail:
        proj_ref, weight_ref, rows_one_ref, x_ref, grad_ref, gain_ref = tail_in
        loads_tail = Loads(zip((weight_ref, rows_one_ref), lazy_tail), lazy_tail[2])
        weight_ref, rows_one_ref = lazy_tail[:2]
    if extra:
        loads_extra = Loads(zip(extra_in[:2], extra_refs), extra_refs[5])
    before = None
    if old_tail:
        before = lazy_old[0]
        loads_old = Loads([(old_qkv[0], before)], lazy_old[1])
    spot = Spot()
    spot.enter(head or last, tail or spreads or extra)
    moving = [Spread(spot, *refs) for refs in zip(spread_in, spread_out, refs)]
    for spread in moving:
        spread.begin()
    if last:
        out_blocks, gains = last_in
        out_target, qkv_target, gain_sum = last_out
        new_qkv, own_gain, all_dp, dp_sum, all_mp, ship_sems, gain_sems, gain_spread_sems = last_refs
        ship_out = Ship(spot, out_blocks, out_target, ship_sems.at[0])
        ship_out.start()
    early, late = [], []
    if extra:
        summed_y = Sum(spot, *extra_refs[:5])
        loads_extra.wait()
        for t in range(spot.places):
            summed_y.sibling(t).start()
        late.append(summed_y)
    if head:
        head_proj_ref, new_out = head_out
        part, got, part_send, part_recv = head_refs[:4]
        made_q, got_q, q_send, q_recv, made_kv, got_kv, kv_send, kv_recv, dq, mix_turned = head_refs[4:]
        pairs = part.shape[0]
        owner_rows = toks * (pairs // heads)
        total = rows_ref.shape[0]
        step = min(512, total)
        loads_head.wait(0)

        @pl.loop(0, total // step)
        def _(i):
            rows = pl.ds(pl.multiple_of(i * step, step), step)
            made = dot_nt(rows_ref[rows, :], out_weight_ref[...]).astype(BF16)
            for j in range(step // owner_rows):
                to = pl.ds(pl.multiple_of((i * (step // owner_rows) + j) * toks, toks), toks)
                for p in range(pairs):
                    s, h = p // heads, p % heads
                    start = j * owner_rows + s * toks
                    part[p, to, :] = made[start : start + toks, h * HEAD : (h + 1) * HEAD]

        swap = Swap(spot, part, got, part_send, part_recv)
        swap.start()

    if extra:

        @pl.loop(0, spot.places - 1)
        def _(s):
            summed_y.begin(s)

    if tail:
        result_ref = tail_out[0]
        sum_refs, (turned, gain_acc) = take(tail_refs, 5)
        if not last:
            new_qkv, gain_acc = tail_out[1:]
        owner_rows = x_ref.shape[0]
        summed = Sum(spot, *sum_refs)
        early.append(summed)
        chip_rows = 2 * owner_rows
        gain_acc[...] = jnp.zeros_like(gain_acc)
        loads_tail.wait()

        @pl.loop(0, spot.places)
        def _(s):
            t = summed.term(s)
            rows = pl.ds(pl.multiple_of(t * chip_rows, chip_rows), chip_rows)
            value = dot_nt(proj_ref[rows, :], weight_ref[...])
            gain_acc[...] += jnp.sum(
                value * rows_one_ref[rows, :].astype(F32), axis=0, keepdims=True
            )
            keep, send = split_cores(spot.core, value.astype(BF16), owner_rows)
            summed.mine[t] = keep[0]
            summed.out[t] = send[0]
            summed.sibling(t).start()
            pl.when(s > 0)(lambda: summed.begin(s - 1))

        if last:
            own_gain[...] = gains[...]
            own_gain[1:2, :] += gain_acc[...]
            gain_dp = Gather(spot, own_gain, lambda index: all_dp.at[index], gain_sems)
            gain_dp.start()
    if last:
        if old_tail:
            loads_old.wait()
        ship_qkv = Ship(spot, new_qkv, qkv_target, ship_sems.at[1])

        def send(i):
            pl.when(i < spot.dp_size - 1)(lambda: ship_qkv.copy(i + 1).start())
            pl.when(i == spot.dp_size - 1)(lambda: ship_qkv.local.start())

        add_grads(spot, rows_one_ref, proj_ref, turned, before, new_qkv, send)
        gain_dp.wait()
        dp_sum[...] = jnp.sum(all_dp[...], axis=0)
        gain_mp = Spread(spot, dp_sum, all_mp, gain_spread_sems)
        gain_mp.begin()
        gain_mp.go_on(1)
    if head:
        add_grads(
            spot, mix_ref, rows_ref, mix_turned, old_out[0] if old_head else None, new_out
        )

    def go_on(hop):
        if hop < spot.places - 1:
            for each in moving + early + late:
                each.go_on(hop)

    if not (tail and head):
        go_on(1)
    if head:
        swap.wait()
        loads_head.wait(1, 2, 3)
        swap_kv = Swap(spot, made_kv, got_kv, kv_send, kv_recv)
        attend_back_blocks(
            spot, qkv, got, ids_ref, cos_ref, sin_ref, made_q, made_kv, dq,
            lambda step: swap_kv.copy(step).start(), lambda: go_on(1 if tail else 2), scale, shift,
        )
        swap_kv.keep()
        swap = Swap(spot, made_q, got_q, q_send, q_recv)
        swap.start()
    for hop in range(2 if tail else 3, spot.places - 1):
        if last:
            gain_mp.go_on(hop)
        go_on(hop)
    if tail and not last:
        if old_tail:
            loads_old.wait()
        add_grads(spot, rows_one_ref, proj_ref, turned, before, new_qkv)
    if head:
        swap_kv.wait()
        swap.wait()
        for o in range(total // owner_rows):
            for p in range(pairs):
                s, h = p // heads, p % heads
                here, there = pl.ds(o * owner_rows + s * toks, toks), pl.ds(o * toks, toks)
                for kind in range(3):
                    piece = (
                        got_kv[p, there, (kind - 1) * HEAD : kind * HEAD] if kind else got_q[p, there, :]
                    )
                    head_proj_ref[
                        here, (kind * heads + h) * HEAD : (kind * heads + h + 1) * HEAD
                    ] = piece
    for spread in moving:
        spread.go_on(spot.places - 1)
    if last and spot.places > 2:
        gain_mp.go_on(spot.places - 1)
    if tail:
        incoming = summed.finish()
        x = x_ref[...].astype(F32)
        term, _ = norm_back(x, norm_factor(x), gain_ref[...], incoming)
        result_ref[...] = grad_ref[...] + term
    if extra:
        extra_out[0][...] = (extra_in[2][...] + summed_y.finish()).astype(BF16)
    if last:
        gain_mp.finish()
        gain_sum[...] = jnp.sum(all_mp[...], axis=0)
        ship_out.wait()
        ship_qkv.wait()
    for spread in moving:
        spread.finish()


def ffn_kernel(
    rows_ref, cot_ref, gate_ref, up_ref, down_ref, y_ref, dh_ref, act_ref, dgate_ref, dup_ref
):
    hidden = gate_ref.shape[1]
    width = rows_ref.shape[1]
    tile = min(256, hidden)

    @pl.loop(0, hidden // tile)
    def _(t):
        cols = pl.ds(pl.multiple_of(t * tile, tile), tile)
        gate = dot(rows_ref[...], gate_ref[:, cols])
        up = dot(rows_ref[...], up_ref[:, cols])
        sig = jax.nn.sigmoid(gate)
        silu = gate * sig
        act_ref[:, cols] = (silu * up).astype(BF16)
        grad = dot_nt(cot_ref[...], down_ref[cols, :])
        dgate_ref[:, cols] = (grad * up * sig * (1.0 + gate * (1.0 - sig))).astype(BF16)
        dup_ref[:, cols] = (grad * silu).astype(BF16)

    @pl.loop(0, width // 256)
    def _(t):
        cols = pl.ds(pl.multiple_of(t * 256, 256), 256)
        y_ref[:, cols] = dot(act_ref[...], down_ref[:, cols]).astype(BF16)
        dh = dot_nt(dgate_ref[...], gate_ref[cols, :]) + dot_nt(dup_ref[...], up_ref[cols, :])
        dh_ref[:, cols] = dh.astype(BF16)


def grad_kernel(count, groups, left_blocked, *refs):
    lefts, refs = take(refs, count)
    rights, refs = take(refs, count * groups)
    out_refs, (turned,) = take(refs, groups)
    rows = lefts[0].shape[0]

    def turn():
        for m, left in enumerate(lefts):
            turned[:, m * rows : (m + 1) * rows] = left[...].T

    if left_blocked:
        turn()
    else:
        pl.when(pl.program_id(0) == 0)(turn)
    tile = math.gcd(out_refs[0].shape[2], 256)
    for g, out_ref in enumerate(out_refs):
        own = rights[g * count : (g + 1) * count]

        @pl.loop(0, out_ref.shape[2] // tile)
        def _(t):
            cols = pl.ds(pl.multiple_of(t * tile, tile), tile)
            total = dot(turned[:, :rows], own[0][:, cols])
            for m in range(1, count):
                total += dot(turned[:, m * rows : (m + 1) * rows], own[m][:, cols])
            out_ref[0, :, cols] = total.astype(BF16)


VMEM = pl.BlockSpec(memory_space=pltpu.VMEM)
ANY = pl.BlockSpec(memory_space=pltpu.HBM)


def cost(flops, nbytes):
    return pl.CostEstimate(flops=flops, bytes_accessed=nbytes, transcendentals=0)


def limits(mebibytes):
    return pltpu.CompilerParams(vmem_limit_bytes=mebibytes * 2**20)


def shape(*dims, dtype=BF16):
    return jax.ShapeDtypeStruct(dims, dtype)


def comm_params(collective_id, mebibytes):
    return pltpu.CompilerParams(
        collective_id=collective_id, has_side_effects=True, vmem_limit_bytes=mebibytes * 2**20
    )


def begin(x, gain, query, key, value, out):
    size, mp_size = lax.axis_size("dp"), lax.axis_size("mp")
    rows, columns = query.shape
    return pl.pallas_call(
        begin_kernel,
        out_shape=[
            shape(rows * size, 3 * columns),
            shape(out.shape[0], out.shape[1] * size),
            shape(mp_size, *x.shape),
        ],
        in_specs=[VMEM] * 2 + [ANY] * 4,
        out_specs=[ANY] * 3,
        scratch_shapes=[
            pltpu.VMEM(x.shape, BF16),
            pltpu.SemaphoreType.DMA((4, 2, size + 1)),
            *spread_scratch(mp_size // 2),
        ],
        compiler_params=comm_params(0, 16),
        cost_estimate=cost(0, 60 * 2**20),
        name="begin",
    )(x, gain, query, key, value, out)


def forward_stage(collective_id, tail, head, norm, shard, gather, heads, toks, scale, shift):
    size, mp_size = lax.axis_size("dp"), lax.axis_size("mp")
    out_shape, scratch = [], []
    if tail:
        blocks, _, x, _ = tail
        owner_rows, width = x.shape
        total = blocks.shape[1] * blocks.shape[0] // heads
        out_shape += [
            shape(owner_rows, width, dtype=F32),
            shape(owner_rows, width),
            shape(total, heads * HEAD),
        ]
        scratch += sum_scratch(mp_size // 2, owner_rows, width)
    if head:
        total, slice_len = head[0].shape[0], head[2].shape[0]
        out_shape += [shape(size, slice_len, 3 * HEAD), shape(size, slice_len, HEAD)]
        scratch += [
            pltpu.VMEM((min(512, total), 3 * heads * HEAD), F32),
            *swap_scratch(size, slice_len, 3 * HEAD),
            *swap_scratch(size, slice_len, HEAD),
        ]
    if norm:
        scratch.append(pltpu.VMEM(norm[0].shape, BF16))
    if head:
        scratch += lazy_scratch(*head[:2])
    here, spreads = len(out_shape), bool(norm) + len(shard)
    out_shape += [shape(mp_size, *array.shape) for array in (*norm[:1], *shard)]
    scratch += spread_scratch(mp_size // 2) * spreads
    axis = None
    if gather:
        weight, axis = gather
        dims = list(weight.shape)
        dims[axis] *= size
        out_shape.append(shape(*dims))
        scratch.append(pltpu.SemaphoreType.DMA((2, size + 1)))
    arrays = [*tail, *head, *norm]
    specs = [VMEM] * len(arrays)
    if head:
        specs[len(tail) : len(tail) + 2] = [ANY] * 2
    return pl.pallas_call(
        functools.partial(
            forward_kernel,
            bool(tail), bool(head), bool(norm), spreads, axis, heads, toks, scale, shift,
        ),
        out_shape=out_shape,
        in_specs=specs + [ANY] * (len(shard) + bool(gather)),
        out_specs=[VMEM] * here + [ANY] * (spreads + bool(gather)),
        scratch_shapes=scratch,
        compiler_params=comm_params(collective_id, 52),
        cost_estimate=cost(10**10, 100 * 2**20),
        name="forward_stage",
    )(*arrays, *shard, *gather[:1])


def middle_part(
    collective_id, defer, ships, rows, cot, weights, middle, local_cot, gain, shards, before
):
    total, width = rows.shape
    gate, _, _, down = weights
    hidden = gate.shape[1]
    size, mp_size = lax.axis_size("dp"), lax.axis_size("mp")
    places = mp_size // 2
    owner_rows = middle.shape[0]
    block = width // size
    wide = [shape(size, block, hidden)] * 2 + [shape(size, hidden, block)]
    half = shape(places, owner_rows, width)
    y_scratch = sum_scratch(places, owner_rows, width)
    if defer:
        y_scratch = [*[pltpu.VMEM(half.shape, BF16)] * 2, pltpu.SemaphoreType.DMA((2,))]
    return pl.pallas_call(
        functools.partial(middle_kernel, not before, defer, ships, len(shards), owner_rows),
        out_shape=[
            shape(owner_rows, width, dtype=F32),
            shape(owner_rows, width),
            shape(1, width, dtype=F32),
            *([half, half] if defer else [shape(owner_rows, width)]),
            *[shape(mp_size, *array.shape) for array in shards],
            *wide,
            *wide[:ships],
        ],
        in_specs=[VMEM] * 3 + [ANY] * (6 + len(shards) + len(before)),
        out_specs=[VMEM] * 3 + ([ANY] * 2 if defer else [VMEM]) + [ANY] * (len(shards) + 3 + ships),
        scratch_shapes=[
            *[pltpu.VMEM((total, hidden), BF16)] * 3,
            pltpu.VMEM((max(block, hidden), total), BF16),
            pltpu.VMEM((2, block, hidden), BF16),
            pltpu.VMEM((hidden, block), BF16),
            pltpu.VMEM((2, block, hidden), BF16),
            pltpu.VMEM((hidden, block), BF16),
            *[pltpu.VMEM(array.shape, BF16) for array in (rows, cot, gate, gate, down)],
            pltpu.SemaphoreType.DMA((4 + 2 * size,)),
            pltpu.SemaphoreType.DMA((2, 3)),
            *sum_scratch(places, owner_rows, width),
            *y_scratch,
            *[pltpu.SemaphoreType.DMA((2, size))] * ships,
            *spread_scratch(places) * len(shards),
        ],
        compiler_params=comm_params(collective_id, 61),
        cost_estimate=cost(18 * total * width * hidden, 60 * 2**20),
        name="middle_part",
    )(middle, local_cot, gain, rows, cot, *weights, *shards, *before)


def backward_stage(
    collective_id, tail, old_qkv, head, old_out, last, extra, shard, heads, toks, scale, shift
):
    size, mp_size = lax.axis_size("dp"), lax.axis_size("mp")
    places = mp_size // 2
    out_shape, scratch = [], []
    if tail:
        owner_rows, width = tail[3].shape
        out_shape.append(shape(owner_rows, width, dtype=F32))
        total = tail[0].shape[0]
        wide = shape(size, width // size, 3 * heads * HEAD)
        if not last:
            out_shape += [wide, shape(1, width, dtype=F32)]
        scratch += [
            *sum_scratch(places, owner_rows, width),
            pltpu.VMEM((width // size, total), BF16),
            pltpu.VMEM((1, width), F32),
        ]
    if head:
        (total, width), slice_len = head[0].shape, head[2].shape[1]
        out_shape.append(shape(total, 3 * heads * HEAD))
        out_shape.append(shape(size, heads * HEAD, width // size))
        scratch += [
            *swap_scratch(size, slice_len, HEAD),
            *swap_scratch(size, slice_len, HEAD),
            *swap_scratch(size, slice_len, 2 * HEAD),
            pltpu.VMEM((size, HEAD, slice_len), F32),
            pltpu.VMEM((heads * HEAD, total), BF16),
        ]
    here = len(out_shape)
    if last:
        gains = last[1].shape
        out_shape += [shape(*last[0].shape), wide]
        scratch += [
            pltpu.VMEM(wide.shape, BF16),
            pltpu.VMEM(gains, F32),
            pltpu.VMEM((size, *gains), F32),
            pltpu.VMEM(gains, F32),
            pltpu.VMEM((mp_size, *gains), F32),
            pltpu.SemaphoreType.DMA((2, 2, size)),
            pltpu.SemaphoreType.DMA((2, size)),
            *spread_scratch(places),
        ]
        out_shape.append(shape(*gains, dtype=F32))
    if extra:
        out_shape.append(shape(*extra[2].shape))
        scratch += sum_scratch(places, *extra[2].shape)
        scratch.append(pltpu.SemaphoreType.DMA((2,)))
    if tail:
        scratch += lazy_scratch(tail[1], tail[2])
    scratch += lazy_scratch(*old_qkv) if old_qkv else []
    if head:
        scratch += lazy_scratch(head[0], head[2], head[4], head[5])
    scratch += spread_scratch(places) * len(shard)
    out_shape += [shape(mp_size, *array.shape) for array in shard]
    arrays = [*tail, *old_qkv, *head, *old_out]
    tail_specs = [VMEM, ANY, ANY, VMEM, VMEM, VMEM] if tail else []
    head_specs = [ANY, VMEM, ANY, VMEM, ANY, ANY, VMEM] if head else []
    specs = [*tail_specs, *[ANY] * len(old_qkv), *head_specs, *[VMEM] * len(old_out)]
    last_specs, last_outs = ([ANY, VMEM], [ANY, ANY, VMEM]) if last else ([], [])
    extra_specs, extra_outs = ([ANY, ANY, VMEM], [VMEM]) if extra else ([], [])
    return pl.pallas_call(
        functools.partial(
            backward_kernel, bool(tail), bool(head), bool(last), len(old_qkv), len(old_out),
            bool(extra), len(shard), heads, toks, scale, shift,
        ),
        out_shape=out_shape,
        in_specs=specs + last_specs + extra_specs + [ANY] * len(shard),
        out_specs=[VMEM] * here + last_outs + extra_outs + [ANY] * len(shard),
        scratch_shapes=scratch,
        compiler_params=comm_params(collective_id, 58),
        cost_estimate=cost(10**10, 100 * 2**20),
        name="backward_stage",
    )(*arrays, *last, *extra, *shard)


def ffn(rows, cot, gate, up, down):
    total, width = rows.shape
    hidden = gate.shape[1]
    step = min(512, total)
    by_rows = pl.BlockSpec((step, width), lambda i: (i, 0))
    by_hidden = pl.BlockSpec((step, hidden), lambda i: (i, 0))
    held = lambda array: pl.BlockSpec(array.shape, lambda i: (0, 0), pipeline_mode=pl.Buffered(1))
    return pl.pallas_call(
        ffn_kernel,
        grid=(total // step,),
        out_shape=[shape(total, width)] * 2 + [shape(total, hidden)] * 3,
        in_specs=[by_rows, by_rows, held(gate), held(up), held(down)],
        out_specs=[by_rows] * 2 + [by_hidden] * 3,
        compiler_params=limits(56),
        cost_estimate=cost(12 * total * width * hidden, 34 * 2**20),
        name="ffn",
    )(rows, cot, gate, up, down)


def weight_grad(lefts, groups, left_blocked):
    count = len(lefts)
    size = lax.axis_size("dp")
    rows = lefts[0].shape[0]
    m, n = lefts[0].shape[1], groups[0][0].shape[1]
    moving = lambda width: pl.BlockSpec((rows, width // size), lambda e: (0, e))
    fixed = lambda width: pl.BlockSpec(
        (rows, width), lambda e: (0, 0), pipeline_mode=pl.Buffered(1)
    )
    left_spec = moving(m) if left_blocked else fixed(m)
    right_spec = fixed(n) if left_blocked else moving(n)
    out = (m // size, n) if left_blocked else (m, n // size)
    return pl.pallas_call(
        functools.partial(grad_kernel, count, len(groups), left_blocked),
        grid=(size,),
        in_specs=[left_spec] * count + [right_spec] * (count * len(groups)),
        out_specs=[pl.BlockSpec((1, *out), lambda e: (e, 0, 0))] * len(groups),
        out_shape=[shape(size, *out)] * len(groups),
        scratch_shapes=[pltpu.VMEM((out[0], count * rows), BF16)],
        compiler_params=limits(52),
        cost_estimate=cost(2 * count * rows * m * n * len(groups), 24 * 2**20),
        name="weight_grad",
    )(*lefts, *(right for group in groups for right in group))


def first_visible(ids):
    at = jnp.arange(ids.shape[-1], dtype=jnp.int32)
    starts = jnp.concatenate([jnp.ones_like(ids[..., :1], jnp.bool_), ids[..., 1:] != ids[..., :-1]], axis=-1)
    return lax.cummax(jnp.where(starts, at, 0), axis=ids.ndim - 1)


def block_at(values, index):
    return lax.dynamic_index_in_dim(values, index, 0, keepdims=False)


def stacked(blocks):
    full = jnp.zeros((len(blocks), *blocks[0].shape), blocks[0].dtype)
    for m, block in enumerate(blocks):
        full = lax.dynamic_update_index_in_dim(full, block, m, 0)
    return full


def scatter_mp(values):
    return lax.psum_scatter(values, "mp", scatter_dimension=0, tiled=True).astype(F32)


def sliced_scores(qkv, kv_all, first, positions, scale, shift):
    raw = jnp.einsum("pqd,pkd->pqk", qkv[..., :HEAD], kv_all[..., :HEAD], preferred_element_type=F32)
    at = jnp.arange(kv_all.shape[1], dtype=jnp.int32)
    visible = (at >= first[..., None]) & (at <= positions[:, None])
    return jnp.where(visible, sigmoid_of(raw, scale, shift), 0.0)


def per_device(
    inputs,
    cotangent,
    doc_ids,
    gain_attn,
    w_query,
    w_key,
    w_value,
    w_out,
    gain_ffn,
    w_gate,
    w_up,
    w_down,
):
    dp_size = lax.axis_size("dp")
    mp_size = lax.axis_size("mp")
    micro_count, row_count, seq_count, width = inputs.shape
    slice_len = row_count * mp_size
    total_len = slice_len * dp_size
    rows_here = row_count * seq_count
    shift = math.log(total_len)
    scale = HEAD ** (-0.5)
    dp_at = lax.axis_index("dp")
    mp_at = lax.axis_index("mp")
    first_row = dp_at * slice_len
    positions = first_row + jnp.arange(slice_len, dtype=jnp.int32)
    head_width = w_query.shape[1]
    heads = head_width // HEAD
    hidden = w_gate.shape[1]
    pairs = seq_count * heads
    whole_pairs = pairs == dp_size
    cos_all, sin_all = full_tables(total_len)
    cos_slice, sin_slice = [
        lax.dynamic_slice_in_dim(table, first_row, slice_len, 0) for table in (cos_all, sin_all)
    ]

    def by_row(table):
        shaped = table.reshape(mp_size, 1, row_count, 1, HEAD)
        return jnp.broadcast_to(shaped, (mp_size, seq_count, row_count, 1, HEAD))

    def rotate(values, back=False):
        sine = -by_row(sin_slice) if back else by_row(sin_slice)
        return values * by_row(cos_slice) + swap_halves(values) * sine

    def to_pairs(values):
        shaped = values.reshape(mp_size, seq_count, row_count, heads, -1)
        return shaped.transpose(1, 3, 0, 2, 4).reshape(pairs, slice_len, -1)

    def from_pairs(values):
        shaped = values.reshape(seq_count, heads, mp_size, row_count, -1)
        return shaped.transpose(2, 0, 3, 1, 4).reshape(mp_size * rows_here, heads, -1)

    def to_rows(values):
        return jnp.swapaxes(values, 0, 1).reshape(rows_here, width)

    def from_rows(values):
        return jnp.swapaxes(values.reshape(seq_count, row_count, width), 0, 1)

    def gather_mp(values):
        return lax.all_gather(values, "mp", axis=0, tiled=True)

    gain_attn_grad = jnp.zeros((width,), F32)
    gain_ffn_grad = jnp.zeros((width,), F32)
    results = []
    input_grads = []
    kept = [[] for _ in range(9)]
    xs = [to_rows(inputs[m]) for m in range(micro_count)]
    cots = [to_rows(cotangent[m]) for m in range(micro_count)]
    micros = range(micro_count)
    if whole_pairs:
        stage = (heads, row_count, scale, shift)
        ids = [
            block_at(doc_ids[m], dp_at // heads).astype(F32).reshape(dp_size, 1, slice_len)
            for m in micros
        ]
        last = micro_count - 1

        def whole(blocks):
            return blocks.reshape(mp_size * rows_here, width)

        def scatter_dp(blocks):
            flat = blocks.reshape(-1, blocks.shape[-1])
            return lax.psum_scatter(flat, "dp", scatter_dimension=0, tiled=True).astype(F32)

        qkv_full, out_full, rows_one = begin(
            xs[0], gain_attn[None], w_query, w_key, w_value, w_out
        )
        cut = w_up.shape[0] // 2
        gathers = {
            0: (w_gate, 0), 1: (w_up[:cut], 0), 2: (w_up[cut:], 0), micro_count: (w_down, 1)
        }
        wide = []
        ones, qkvs, got, middles, lows, twos, mixtures = [whole(rows_one)], [], [], [], [], [], []
        for m in range(micro_count + 1):
            tail, head, norm, shard = (), (), (), ()
            if m:
                tail = (got[m - 1], out_full, xs[m - 1], gain_ffn[None])
            if m < micro_count:
                head = (ones[m], qkv_full, cos_slice, sin_slice, ids[m])
            if m < last:
                norm = (xs[m + 1], gain_attn[None])
            elif lows:
                shard = (lows[m - last],)
            if m == 0:
                shard += (cots[0],)
            outs = forward_stage(10 + m, tail, head, norm, shard, gathers.get(m, ()), *stage)
            if tail:
                (middle, low, mixture), outs = take(outs, 3)
                middles.append(middle)
                lows.append(low)
                mixtures.append(mixture)
            if head:
                (qkv, block), outs = take(outs, 2)
                qkvs.append(qkv)
                got.append(block)
            if norm or shard:
                (ones if m < last else twos).append(whole(outs[0]))
            if m == 0:
                portions = [whole(outs[1])]
            if m in gathers:
                wide.append(outs[-1])
        grads, low_grads, attns, projs, sums, gain_parts, later = [], [], [], [], [], [], []
        for m in micros:
            shard = (lows[len(twos)] if len(twos) < micro_count else low_grads[len(attns)],)
            if m < last:
                shard += (cots[m + 1],)
            defer = m == 0
            grad, low, gain_part, *others = middle_part(
                30 + m, defer, int(m == last), twos[m], portions[m], wide, middles[m], cots[m], gain_ffn[None],
                shard, sums,
            )
            ys, (full, *others) = take(others, 2 if defer else 1)
            later.append((*ys, middles[m]) if defer else ys)
            (twos if len(twos) < micro_count else attns).append(whole(full))
            if m < last:
                portions.append(whole(others[0]))
            sums, gate_blocks = take(others[m < last :], 3)
            grads.append(grad)
            low_grads.append(low)
            gain_parts.append(gain_part)
        sum_up, sum_down = [scatter_dp(blocks) for blocks in sums[1:]]
        sum_gate = jnp.sum(gate_blocks[0].astype(F32), axis=0)
        old_qkv, old_out, attn_parts, finished = (), (), [], list(later)
        for m in range(micro_count + 1):
            tail, head, shard, final = (), (), (), ()
            if m:
                tail = (projs[m - 1], qkv_full, ones[m - 1], xs[m - 1], grads[m - 1], gain_attn[None])
            if m < micro_count:
                head = (attns[m], out_full, qkvs[m], ids[m], cos_all, sin_all, mixtures[m])
            else:
                rows = [sum(gain_parts), sum(attn_parts), jnp.zeros((6, width), F32)]
                final = (*old_out, jnp.concatenate(rows, axis=0))
            if len(attns) < micro_count:
                shard = (low_grads[len(attns)],)
            extra = later[0] if m == 0 else ()
            outs = backward_stage(
                20 + m, tail, old_qkv, head, () if final else old_out, final, extra, shard, *stage
            )
            if tail:
                (input_grad,), outs = take(outs, 1)
                input_grads.append(from_rows(input_grad))
            if tail and head:
                (new_qkv, gain_part), outs = take(outs, 2)
                old_qkv = (new_qkv,)
                attn_parts.append(gain_part)
            if head:
                (proj, new_out), outs = take(outs, 2)
                projs.append(proj)
                old_out = (new_out,)
            if extra:
                finished[0] = outs[:1]
            if shard:
                attns.append(whole(outs[-1]))
        results = [from_rows(result[0]) for result in finished]
        sum_out, sum_qkv = (jnp.sum(blocks.astype(F32), axis=0) for blocks in outs[:2])
        gain_sums = (outs[2][1] / gain_attn, outs[2][0])
    else:
        qkv_full = lax.all_gather(
            jnp.concatenate([w_query, w_key, w_value], axis=1), "dp", axis=0, tiled=True
        )
        out_full = lax.all_gather(w_out, "dp", axis=1, tiled=True)
        gate_full = lax.all_gather(w_gate, "dp", axis=0, tiled=True)
        up_full = lax.all_gather(w_up, "dp", axis=0, tiled=True)
        down_full = lax.all_gather(w_down, "dp", axis=1, tiled=True)
        first_all = first_visible(doc_ids)
        normed = [
            (x.astype(F32) * norm_factor(x.astype(F32)) * gain_attn).astype(BF16) for x in xs
        ]
        for micro in micros:
            local_rows = xs[micro].astype(F32)
            local_cot = cots[micro]
            factor_one = norm_factor(local_rows)
            rows_one = gather_mp(normed[micro])
            portion = gather_mp(local_cot)
            projected = dot(rows_one, qkv_full).reshape(
                mp_size, seq_count, row_count, 3, heads, HEAD
            )
            packed = to_pairs(
                jnp.concatenate(
                    [
                        rotate(projected[:, :, :, 0]).astype(BF16),
                        rotate(projected[:, :, :, 1]).astype(BF16),
                        projected[:, :, :, 2].astype(BF16),
                    ],
                    axis=-1,
                )
            )
            kv_all = lax.all_gather(packed[..., HEAD:], "dp", axis=1, tiled=True)
            first = lax.dynamic_slice_in_dim(first_all[micro], first_row, slice_len, 1)
            first = jnp.repeat(first, heads, axis=0)
            weights = sliced_scores(packed, kv_all, first, positions, scale, shift)
            attended = jnp.einsum(
                "pqk,pkd->pqd", weights.astype(BF16), kv_all[..., HEAD:], preferred_element_type=F32
            ).astype(BF16)
            mixture = from_pairs(attended).reshape(mp_size * rows_here, head_width)
            middle = local_rows + scatter_mp(dot(mixture, out_full).astype(BF16))
            factor_two = norm_factor(middle)
            rows_two = gather_mp((middle * factor_two * gain_ffn).astype(BF16))
            y, dh, activated, gate_grad, up_grad = ffn(
                rows_two, portion, gate_full, up_full, down_full
            )
            results.append(from_rows((middle + scatter_mp(y)).astype(BF16)))
            middle_term, gain_part = norm_back(middle, factor_two, gain_ffn, scatter_mp(dh))
            gain_ffn_grad = gain_ffn_grad + gain_part
            middle_grad = local_cot.astype(F32) + middle_term
            attn_portion = gather_mp(middle_grad.astype(BF16))
            mix_grad = to_pairs(dot_nt(attn_portion, out_full).astype(BF16))
            sig = sliced_scores(packed, kv_all, first, positions, scale, shift)
            prob_grad = jnp.einsum(
                "pqd,pkd->pqk", mix_grad, kv_all[..., HEAD:], preferred_element_type=F32
            )
            score_grad = (prob_grad * sig * (1.0 - sig)).astype(BF16)
            dq = jnp.einsum("pqk,pkd->pqd", score_grad, kv_all[..., :HEAD], preferred_element_type=F32)
            dk = jnp.einsum("pqk,pqd->pkd", score_grad, packed[..., :HEAD], preferred_element_type=F32)
            dv = jnp.einsum("pqk,pqd->pkd", sig.astype(BF16), mix_grad, preferred_element_type=F32)
            dkv = lax.psum_scatter(
                jnp.concatenate([dk * scale, dv], axis=-1).astype(BF16), "dp", scatter_dimension=1, tiled=True
            ).astype(F32)
            back = from_pairs(jnp.concatenate([dq * scale, dkv], axis=-1))
            back = back.reshape(mp_size, seq_count, row_count, heads, 3 * HEAD)
            proj_grad = jnp.stack(
                [
                    rotate(back[..., :HEAD], True),
                    rotate(back[..., HEAD : 2 * HEAD], True),
                    back[..., 2 * HEAD :],
                ],
                axis=3,
            ).astype(BF16).reshape(mp_size * rows_here, 3 * head_width)
            partial_grad = dot_nt(proj_grad, qkv_full)
            gain_attn_grad = gain_attn_grad + jnp.sum(partial_grad * rows_one.astype(F32), axis=0)
            input_term, _ = norm_back(
                local_rows, factor_one, gain_attn, scatter_mp(partial_grad.astype(BF16))
            )
            input_grads.append(from_rows(middle_grad + input_term))
            for held, array in zip(
                kept,
                (rows_one, proj_grad, mixture, attn_portion, rows_two, gate_grad, up_grad, activated, portion),
            ):
                held.append(array)

        def scatter_dp(lefts, rights, left_blocked):
            (blocks,) = weight_grad(lefts, (rights,), left_blocked)
            return lax.psum_scatter(blocks, "dp", scatter_dimension=0, tiled=True)[0].astype(F32)

        ones, projs, mixtures, attns, twos, gates, ups, acts, portions = kept
        sum_gate = scatter_dp(twos, gates, True)
        sum_up = scatter_dp(twos, ups, True)
        sum_down = scatter_dp(acts, portions, False)
        sum_out = scatter_dp(mixtures, attns, False)
        sum_qkv = scatter_dp(ones, projs, True)
        gain_sums = lax.psum((gain_attn_grad / gain_attn, gain_ffn_grad), ("dp", "mp"))
    return (
        stacked(results),
        stacked(input_grads),
        gain_sums[0],
        sum_qkv[:, :head_width],
        sum_qkv[:, head_width : 2 * head_width],
        sum_qkv[:, 2 * head_width :],
        sum_out,
        gain_sums[1],
        sum_gate,
        sum_up,
        sum_down,
    )


def solution(mesh):
    tokens = P(None, ("dp", "mp"), None, None)
    column = P("dp", "mp")
    row = P("mp", "dp")
    return jax.shard_map(
        per_device,
        mesh=mesh,
        in_specs=(
            tokens, tokens, P(), P(), column, column, column, row, P(), column, column, row,
        ),
        out_specs=(
            tokens, tokens, P(), column, column, column, row, P(), column, column, row,
        ),
        check_vma=False,
    )
```

profile of v0, /device:TPU:0, one launch (start us, length us, event | category | flops | bytes accessed | tf_op | source)
XLA Modules:
  0.0 938.8 jit_solution(11239523161604910204)
XLA Ops:
  7.2 0.0 reduce-scatter.3.cloned.1.call-start
  7.2 2.4 slice_bitcast_fusion.2
  9.7 0.2 copy.25
  9.8 0.0 copy-start
  9.9 0.0 copy-start.27
  9.9 0.2 copy.26
  10.1 0.0 copy-start.1
  10.1 2.9 slice_bitcast_fusion
  13.0 1.0 copy.27
  13.9 1.0 copy.28
  14.9 1.0 fusion.1
  15.9 1.0 copy.29
  16.9 1.0 copy.30
  17.9 1.1 constant_dynamic-slice_fusion
  19.1 44.3 %begin.1 = (bf16[2048,768]{1,0:T(8,128)(2,1)S(1)}, bf16[256,2048]{1,0:T(8,128)(2,1)S(1)}, bf16[8,128,2048]{2,1,0:T(8,128)(2,1)S(1)}) custom-call(bf16[128,2048]{1,0:T(8,128)(2,1)S(1)} %bitcast.83, f32[1,2048]{1,0:T(1,128)S(1)} %bitcast.92, bf16[512,256]{1,0:T(8,128)(2,1)S(1)} %copy-done.2, bf16[512,256]{1,0:T(8,128)(2,1)S(1)} %copy-done.3, ...), custom_call_target="tpu_custom_call" | custom-call | bytes 62914560 | tf_op jit(solution)/shard_map/begin/pallas_call | solution.py:1171
  63.4 2.0 copy-done.11
  65.4 1.7 copy-done.12
  67.1 77.2 %forward_stage.4 = (bf16[4,512,384]{2,1,0:T(8,128)(2,1)}, bf16[4,512,128]{2,1,0:T(8,128)(2,1)S(1)}, bf16[8,128,2048]{2,1,0:T(8,128)(2,1)}, bf16[8,128,2048]{2,1,0:T(8,128)(2,1)}, bf16[2048,1024]{1,0:T(8,128)(2,1)}) custom-call(bf16[1024,2048]{1,0:T(8,128)(2,1)} %bitcast.101, bf16[2048,768]{1,0:T(8,128)(2,1)} %copy-done.12, ...), custom_call_target="tpu_custom_call" | custom-call | flops 10000000000 | bytes 104857600 | tf_op jit(solution)/shard_map/forward_stage/pallas_call | solution.py:1230
  144.3 0.0 copy-start.19
  144.3 0.8 copy-done.19
  145.1 62.7 %forward_stage.5 = (f32[128,2048]{1,0:T(8,128)}, bf16[128,2048]{1,0:T(8,128)(2,1)S(1)}, bf16[1024,256]{1,0:T(8,128)(2,1)S(1)}, bf16[4,512,384]{2,1,0:T(8,128)(2,...) custom-call(bf16[4,512,128]{2,1,0:T(8,128)(2,1)} %copy-done.19, ...), custom_call_target="tpu_custom_call" | custom-call | flops 10000000000 | bytes 104857600 | tf_op jit(solution)/shard_map/forward_stage/pallas_call | solution.py:1230
  207.8 0.8 copy-done.18
  208.6 59.7 %forward_stage.6 = (f32[128,2048]{1,0:T(8,128)}, bf16[128,2048]{1,0:T(8,128)(2,1)S(1)}, bf16[1024,256]{1,0:T(8,128)(2,1)S(1)}, bf16[4,512,384]{2,1,0:T(8,128)(2,...) custom-call(bf16[4,512,128]{2,1,0:T(8,128)(2,1)} %get-tuple-element.88.refs_0_, ...), custom_call_target="tpu_custom_call" | custom-call | flops 10000000000 | bytes 104857600 | tf_op jit(solution)/shard_map/forward_stage/pallas_call | solution.py:1230
  268.3 0.0 copy-start.16
  268.3 0.8 copy-done.16
  269.1 0.8 copy-done.20
  269.9 1.0 copy-done.21
  270.9 52.8 %forward_stage.7 = (f32[128,2048]{1,0:T(8,128)}, bf16[128,2048]{1,0:T(8,128)(2,1)S(1)}, bf16[1024,256]{1,0:T(8,128)(2,1)S(1)}, bf16[8,128,2048]{2,1,0:T(8,128)(2,1)}, bf16[1024,2048]{1,0:T(8,128)(2,1)}) custom-call(bf16[4,512,128]{2,1,0:T(8,128)(2,1)S(1)} %copy-done.21, bf16[256,2048]{1,0:T(8,128)(2,1)} %copy-done.13, bf16[128,2048]{1,0:T(8,128)(2,1)} %bitcast.117, ...), custom_call_target="tpu_custom_call" | custom-call | flops 10000000000 | bytes 104857600 | tf_op jit(solution)/shard_map/forward_stage/pallas_call | solution.py:1230
  323.7 0.8 copy-done.15
  324.5 0.8 copy-done.22
  325.3 91.0 %middle_part.3 = (f32[128,2048]{1,0:T(8,128)}, bf16[128,2048]{1,0:T(8,128)(2,1)}, f32[1,2048]{1,0:T(1,128)}, bf16[4,128,2048]{2,1,0:T(8,128)(2,1)}, bf16[4,128,2...) custom-call(f32[128,2048]{1,0:T(8,128)} %get-tuple-element.95.middle, ...), custom_call_target="tpu_custom_call" | custom-call | flops 38654705664 | bytes 62914560 | tf_op jit(solution)/shard_map/middle_part/pallas_call | solution.py:1260
  416.3 107.7 %middle_part.4 = (f32[128,2048]{1,0:T(8,128)}, bf16[128,2048]{1,0:T(8,128)(2,1)}, f32[1,2048]{1,0:T(1,128)}, bf16[128,2048]{1,0:T(8,128)(2,1)}, bf16[8,128,2048]...) custom-call(f32[128,2048]{1,0:T(8,128)} %get-tuple-element.91.middle, ...), custom_call_target="tpu_custom_call" | custom-call | flops 38654705664 | bytes 62914560 | tf_op jit(solution)/shard_map/middle_part/pallas_call | solution.py:1260
  524.0 112.4 %middle_part.5 = (f32[128,2048]{1,0:T(8,128)}, bf16[128,2048]{1,0:T(8,128)(2,1)}, f32[1,2048]{1,0:T(1,128)}, bf16[128,2048]{1,0:T(8,128)(2,1)}, bf16[8,128,2048]...) custom-call(f32[128,2048]{1,0:T(8,128)} %get-tuple-element.113.middl, ...), custom_call_target="tpu_custom_call" | custom-call | flops 38654705664 | bytes 62914560 | tf_op jit(solution)/shard_map/middle_part/pallas_call | solution.py:1260
  636.4 0.0 reduce-scatter.3.cloned.1.call-update
  636.4 0.0 reduce-scatter.5.cloned.1.call-start
  636.5 0.7 reduce-scatter.5.cloned.1.call-update
  637.2 81.7 %backward_stage.4 = (bf16[1024,768]{1,0:T(8,128)(2,1)}, bf16[4,256,512]{2,1,0:T(8,128)(2,1)}, bf16[128,2048]{1,0:T(8,128)(2,1)}, bf16[8,128,2048]{2,1,0:T(8,128)(2,1)}) custom-call(bf16[1024,2048]{1,0:T(8,128)(2,1)} %bitcast.135, bf16[256,2048]{1,0:T(8,128)(2,1)} %copy-done.13, bf16[4,512,384]{2,1,0:T(8,128)(2,1)} %get-tuple-element.109.refs_2_, ...), custom_call_target="tpu_custom_call" | custom-call | flops 10000000000 | bytes 104857600 | tf_op jit(solution)/shard_map/backward_stage/pallas_call | solution.py:1355
  718.8 1.7 copy.44
  720.6 55.9 %backward_stage.5 = (f32[128,2048]{1,0:T(8,128)}, bf16[4,512,768]{2,1,0:T(8,128)(2,1)}, f32[1,2048]{1,0:T(1,128)}, bf16[1024,768]{1,0:T(8,128)(2,1)}, bf16[4,256,512]{2,1,0:T(8,128)(2,1)}) custom-call(bf16[1024,768]{1,0:T(8,128)(2,1)} %get-tuple-element.124.refs_0_, bf16[2048,768]{1,0:T(8,128)(2,1)} %copy-done.12, bf16[1024,2048]{1,0:T(8,128)(2,1)} %bitcast.102, ...), custom_call_target="tpu_custom_call" | custom-call | flops 10000000000 | bytes 104857600 | tf_op jit(solution)/shard_map/backward_stage/pallas_call | solution.py:1355
  776.4 2.0 copy.43
  778.5 1.5 dynamic_update_slice.23
  780.0 55.5 %backward_stage.6 = (f32[128,2048]{1,0:T(8,128)}, bf16[4,512,768]{2,1,0:T(8,128)(2,1)}, f32[1,2048]{1,0:T(1,128)}, bf16[1024,768]{1,0:T(8,128)(2,1)}, bf16[4,256,512]{2,1,0:T(8,128)(2,1)}) custom-call(bf16[1024,768]{1,0:T(8,128)(2,1)} %get-tuple-element.131.refs_0_, bf16[2048,768]{1,0:T(8,128)(2,1)} %copy-done.12, bf16[1024,2048]{1,0:T(8,128)(2,1)} %bitcast.133, ...), custom_call_target="tpu_custom_call" | custom-call | flops 10000000000 | bytes 104857600 | tf_op jit(solution)/shard_map/backward_stage/pallas_call | solution.py:1355
  835.5 0.7 add.40
  836.3 0.1 pad.4.clone
  836.4 0.7 maximum_maximum_fusion.refs_8_
  837.1 74.3 %backward_stage.7 = (f32[128,2048]{1,0:T(8,128)}, bf16[4,256,512]{2,1,0:T(8,128)(2,1)}, bf16[4,512,768]{2,1,0:T(8,128)(2,1)}, f32[8,2048]{1,0:T(8,128)}) custom-call(bf16[1024,768]{1,0:T(8,128)(2,1)} %get-tuple-element.139.refs_0_, bf16[2048,768]{1,0:T(8,128)(2,1)} %copy-done.12, bf16[1024,2048]{1,0:T(8,128)(2,1)} %bitcast.131, bf16[128,2048]{1,0:T(8,128)(2,1)} %bitcast.118, ...), custom_call_target="tpu_custom_call" | custom-call | flops 10000000000 | bytes 104857600 | tf_op jit(solution)/shard_map/backward_stage/pallas_call | solution.py:1355
  911.4 1.6 fusion.2
  913.1 0.6 div.16
  913.7 0.9 dynamic_update_slice.20
  914.6 2.2 convert_reduce_fusion.2
  916.8 0.4 convert_reduce_fusion.1
  917.3 1.2 fusion
  918.4 1.1 copy-done.23
  919.6 2.3 convert_reduce_fusion
  921.9 0.6 bitcast_dynamic-update-slice_fusion.3
  922.4 0.6 bitcast_dynamic-update-slice_fusion.2
  923.0 0.0 copy-start.26
  923.0 0.9 bitcast_dynamic-update-slice_fusion.1
  923.9 0.2 copy-done.26
  924.2 0.9 bitcast_dynamic-update-slice_fusion
  925.0 0.0 copy-start.24
  925.1 0.0 reduce-scatter.3.cloned.1.call-done
  925.1 3.6 convert_element_type.63
  928.7 2.8 convert_element_type.64
  (62 shorter events, 0.2 us)
Async XLA Ops:
  7.2 2.7 copy-start.32
  7.2 917.9 %reduce-scatter.3.cloned.1.call-start = ((), (), s32[]{:S(2)}) async-start(), calls=%async_computation.2 | async-start | bytes 5242880 | tf_op jit(solution)/shard_map/reduce_scatter | solution.py:1524
  9.8 9.2 copy-start
  9.9 5.0 copy-start.27
  10.1 57.0 %copy-start.1 = (bf16[2,64,2048]{2,1,0:T(8,128)(2,1)}, bf16[2,64,2048]{2,1,0:T(8,128)(2,1)S(1)}, u32[]{:S(2)}) copy-start(bf16[2,64,2048]{2,1,0:T(8,128)(2,1)S(1)} %copy.26) | copy-start | bytes 1572868
  13.9 5.1 copy-start.2
  13.9 5.1 copy-start.3
  13.9 5.1 copy-start.4
  13.9 5.1 copy-start.5
  13.9 5.1 copy-start.6
  17.9 126.4 %copy-start.8 = (f32[1,1,2048]{2,1,0:T(1,128)}, f32[1,1,2048]{2,1,0:T(1,128)S(1)}, u32[]{:S(2)}) copy-start(f32[1,1,2048]{2,1,0:T(1,128)S(1)} %dynamic-slice_convert_fusion.2) | copy-start | bytes 24580
  17.9 127.1 %copy-start.10 = (f32[1,1,2048]{2,1,0:T(1,128)}, f32[1,1,2048]{2,1,0:T(1,128)S(1)}, u32[]{:S(2)}) copy-start(f32[1,1,2048]{2,1,0:T(1,128)S(1)} %get-tuple-element.174) | copy-start | bytes 24580
  17.9 190.6 %copy-start.9 = (f32[1,1,2048]{2,1,0:T(1,128)}, f32[1,1,2048]{2,1,0:T(1,128)S(1)}, u32[]{:S(2)}) copy-start(f32[1,1,2048]{2,1,0:T(1,128)S(1)} %get-tuple-element.173) | copy-start | bytes 24580
  63.3 2.1 copy-start.11
  65.4 1.7 copy-start.12
  67.1 77.2 %copy-start.13 = (bf16[256,2048]{1,0:T(8,128)(2,1)}, bf16[256,2048]{1,0:T(8,128)(2,1)S(1)}, u32[]{:S(2)}) copy-start(bf16[256,2048]{1,0:T(8,128)(2,1)S(1)} %get-tuple-element.86.refs_1_.refs_7_.refs_8_) | copy-start | bytes 3145732
  67.1 78.0 %copy-start.14 = (f32[2048]{0:T(1024)S(1)}, f32[2048]{0:T(1024)}, u32[]{:S(2)}) copy-start(f32[2048]{0:T(1024)} %param.22) | copy-start | bytes 24580
  144.3 0.8 copy-start.19
  207.8 0.8 copy-start.18
  208.6 59.7 %copy-start.17 = (bf16[1024,256]{1,0:T(8,128)(2,1)}, bf16[1024,256]{1,0:T(8,128)(2,1)S(1)}, u32[]{:S(2)}) copy-start(bf16[1024,256]{1,0:T(8,128)(2,1)S(1)} %get-tuple-element.110.refs_6_) | copy-start | bytes 1572868
  268.3 0.8 copy-start.16
  269.1 0.8 copy-start.20
  269.8 1.0 copy-start.21
  323.7 0.8 copy-start.15
  324.5 0.8 copy-start.22
  636.4 292.2 %reduce-scatter.5.cloned.1.call-start = ((), (), s32[]{:S(2)}) async-start(), calls=%async_computation.3 | async-start | bytes 5242880 | tf_op jit(solution)/shard_map/reduce_scatter | solution.py:1524
  780.0 55.6 %copy-start.33 = (f32[1,2048]{1,0:T(1,128)S(1)}, f32[1,2048]{1,0:T(1,128)}, u32[]{:S(2)}) copy-start(f32[1,2048]{1,0:T(1,128)} %get-tuple-element.146) | copy-start | bytes 24580
  780.0 56.4 %copy-start.34 = (f32[1,2048]{1,0:T(1,128)S(1)}, f32[1,2048]{1,0:T(1,128)}, u32[]{:S(2)}) copy-start(f32[1,2048]{1,0:T(1,128)} %get-tuple-element.143) | copy-start | bytes 24580
  780.0 56.4 %copy-start.35 = (f32[1,2048]{1,0:T(1,128)S(1)}, f32[1,2048]{1,0:T(1,128)}, u32[]{:S(2)}) copy-start(f32[1,2048]{1,0:T(1,128)} %get-tuple-element.144) | copy-start | bytes 24580
  780.0 56.4 %copy-start.36 = (f32[1,2048]{1,0:T(1,128)S(1)}, f32[1,2048]{1,0:T(1,128)}, u32[]{:S(2)}) copy-start(f32[1,2048]{1,0:T(1,128)} %get-tuple-element.145) | copy-start | bytes 24580
  837.1 76.0 %copy-start.7 = (f32[2048]{0:T(1024)S(1)}, f32[2048]{0:T(1024)}, u32[]{:S(2)}) copy-start(f32[2048]{0:T(1024)} %param.17) | copy-start | bytes 24580
  911.4 5.4 copy-start.25
  916.8 2.8 copy-start.23
  919.6 2.3 copy-start.30
  919.6 2.8 copy-start.31
  919.6 3.4 copy-start.28
  921.8 2.3 copy-start.29
  923.0 1.1 copy-start.26
  925.0 6.5 copy-start.24
Sparse Core Ops, SparseCore 0:
  636.5 102.8 reduce-scatter.2
  742.7 73.8 reduce-scatter.4
where the time goes:
time: 948 us; the launch traced here: 939 us
  Pallas kernels  875 us (92%)
  local copies, waits for them, and re-layouts  34.5 us (4%)
  between operations  15 us (2%)
  other arithmetic  13.4 us (1%)
    pallas_call x3, Pallas kernels, middle_part(): pl.pallas_call(functools.partial(middle_kernel, not before, defer, ships,...  311 us
    pallas_call x4, Pallas kernels, backward_stage(): pl.pallas_call(functools.partial(backward_kernel, bool(tail), bool(head),...  267 us
    pallas_call x4, Pallas kernels, forward_stage(): pl.pallas_call(functools.partial(forward_kernel, bool(tail), bool(head),...  252 us
    pallas_call x1, Pallas kernels, begin(): pl.pallas_call(begin_kernel, out_shape=[shape(rows * size, 3 * columns),...  44.3 us
  transfers between devices with their start and end apart: 2, of which 0 were waited for; matrix products, arithmetic and copies ran while one was open for 2% of the time, Pallas kernels for 28%

commit v1 on v0

--- a/solution.py
+++ b/solution.py
@@ -749,6 +749,11 @@
             load(g, spot.peer(1)).start()
     loads.wait()
 
+    def go_on(chains, hop):
+        if hop < spot.places - 1:
+            for each in chains:
+                each.go_on(hop)
+
     @pl.loop(0, spot.places)
     def _(s):
         place = summed.term(s)
@@ -771,14 +776,8 @@
                 for each in sums:
                     each.begin(s - 1)
 
-        for hop in range(1, spot.places - 1):
-
-            @pl.when(s == hop + 1)
-            def _():
-                for spread in moving:
-                    spread.go_on(hop)
-                for each in sums:
-                    each.go_on(hop)
+        pl.when(s == 2)(lambda: go_on(moving, 1))
+        pl.when(s == 3)(lambda: go_on(sums[:1], 1))
 
         @pl.loop(0, width // 256)
         def _(t):
@@ -799,6 +798,10 @@
     if defer:
         for copy in stores:
             copy.start()
+    if spot.places == 3:
+        go_on(sums[:1], 1)
+    go_on(moving, 2)
+    go_on(sums[1:], 1)
 
     def send(i):
         if ships:
@@ -832,6 +835,8 @@
 
     @pl.loop(0, blocks)
     def _(i):
+        pl.when(i == 1)(lambda: go_on(sums[:1], 2))
+        pl.when(i == blocks - 1)(lambda: go_on(sums[1:], 2))
         left = turned.at[pl.ds(0, block), :]
         at = spot.peer(i + 1) * block
         left[...] = rows_ref[:, pl.ds(pl.multiple_of(at, block), block)].T
@@ -841,6 +846,8 @@
     if ships:
         store(0, spot.dp).wait()
         send(blocks - 1)
+    for hop in range(3, spot.places - 1):
+        go_on(moving + sums, hop)
     for spread in moving:
         spread.go_on(spot.places - 1)
     left = turned.at[pl.ds(0, hidden), :]

time: 948 us -> 907 us (0.957)
  Pallas kernels: 875 us -> 834 us
    pallas_call x3, Pallas kernels: 311 us -> 289 us  [middle_part(): pl.pallas_call(functools.partial(middle_kernel, not before, defer, ships,...]
    pallas_call x4, Pallas kernels: 267 us -> 249 us  [backward_stage(): pl.pallas_call(functools.partial(backward_kernel, bool(tail), bool(head),...]
  transfers between devices with their start and end apart: 2 -> 2, of which waited for: 0 -> 0; matrix products, arithmetic and copies ran while one was open for 2% -> 3% of each run, Pallas kernels for 28% -> 28%
where the time goes in v1:
time: 907 us; the launch traced here: 898 us
  Pallas kernels  834 us (92%)
  local copies, waits for them, and re-layouts  34.5 us (4%)
  between operations  14.8 us (2%)
  other arithmetic  13.4 us (1%)
    pallas_call x3, Pallas kernels, middle_part(): pl.pallas_call(functools.partial(middle_kernel, not before, defer, ships,...  289 us
    pallas_call x4, Pallas kernels, forward_stage(): pl.pallas_call(functools.partial(forward_kernel, bool(tail), bool(head),...  252 us
    pallas_call x4, Pallas kernels, backward_stage(): pl.pallas_call(functools.partial(backward_kernel, bool(tail), bool(head),...  249 us
    pallas_call x1, Pallas kernels, begin(): pl.pallas_call(begin_kernel, out_shape=[shape(rows * size, 3 * columns),...  44.3 us
  transfers between devices with their start and end apart: 2, of which 0 were waited for; matrix products, arithmetic and copies ran while one was open for 3% of the time, Pallas kernels for 28%

profile of v1, /device:TPU:0, one launch (start us, length us, event | category | flops | bytes accessed | tf_op | source)
XLA Modules:
  0.0 897.9 jit_solution(11483522840689714067)
XLA Ops:
  7.2 0.0 reduce-scatter.3.cloned.1.call-start
  7.2 2.4 slice_bitcast_fusion.2
  9.7 0.2 copy.25
  9.8 0.0 copy-start
  9.9 0.0 copy-start.27
  9.9 0.2 copy.26
  10.1 0.0 copy-start.1
  10.1 2.9 slice_bitcast_fusion
  13.0 1.0 copy.27
  13.9 0.0 copy-start.6
  13.9 1.0 copy.28
  14.9 1.0 fusion.1
  15.9 1.0 copy.29
  16.9 1.0 copy.30
  17.9 0.0 copy-start.8
  17.9 1.1 constant_dynamic-slice_fusion
  19.1 44.3 %begin.1 = (bf16[2048,768]{1,0:T(8,128)(2,1)S(1)}, bf16[256,2048]{1,0:T(8,128)(2,1)S(1)}, bf16[8,128,2048]{2,1,0:T(8,128)(2,1)S(1)}) custom-call(bf16[128,2048]{1,0:T(8,128)(2,1)S(1)} %bitcast.83, f32[1,2048]{1,0:T(1,128)S(1)} %bitcast.92, bf16[512,256]{1,0:T(8,128)(2,1)S(1)} %copy-done.2, bf16[512,256]{1,0:T(8,128)(2,1)S(1)} %copy-done.3, ...), custom_call_target="tpu_custom_call" | custom-call | bytes 62914560 | tf_op jit(solution)/shard_map/begin/pallas_call | solution.py:1178
  63.4 2.0 copy-done.11
  65.4 1.7 copy-done.12
  67.1 77.2 %forward_stage.4 = (bf16[4,512,384]{2,1,0:T(8,128)(2,1)}, bf16[4,512,128]{2,1,0:T(8,128)(2,1)S(1)}, bf16[8,128,2048]{2,1,0:T(8,128)(2,1)}, bf16[8,128,2048]{2,1,0:T(8,128)(2,1)}, bf16[2048,1024]{1,0:T(8,128)(2,1)}) custom-call(bf16[1024,2048]{1,0:T(8,128)(2,1)} %bitcast.101, bf16[2048,768]{1,0:T(8,128)(2,1)} %copy-done.12, ...), custom_call_target="tpu_custom_call" | custom-call | flops 10000000000 | bytes 104857600 | tf_op jit(solution)/shard_map/forward_stage/pallas_call | solution.py:1237
  144.3 0.0 copy-start.19
  144.3 0.8 copy-done.19
  145.1 62.5 %forward_stage.5 = (f32[128,2048]{1,0:T(8,128)}, bf16[128,2048]{1,0:T(8,128)(2,1)S(1)}, bf16[1024,256]{1,0:T(8,128)(2,1)S(1)}, bf16[4,512,384]{2,1,0:T(8,128)(2,...) custom-call(bf16[4,512,128]{2,1,0:T(8,128)(2,1)} %copy-done.19, ...), custom_call_target="tpu_custom_call" | custom-call | flops 10000000000 | bytes 104857600 | tf_op jit(solution)/shard_map/forward_stage/pallas_call | solution.py:1237
  207.6 0.0 copy-start.18
  207.6 0.8 copy-done.18
  208.4 59.7 %forward_stage.6 = (f32[128,2048]{1,0:T(8,128)}, bf16[128,2048]{1,0:T(8,128)(2,1)S(1)}, bf16[1024,256]{1,0:T(8,128)(2,1)S(1)}, bf16[4,512,384]{2,1,0:T(8,128)(2,...) custom-call(bf16[4,512,128]{2,1,0:T(8,128)(2,1)} %get-tuple-element.88.refs_0_, ...), custom_call_target="tpu_custom_call" | custom-call | flops 10000000000 | bytes 104857600 | tf_op jit(solution)/shard_map/forward_stage/pallas_call | solution.py:1237
  268.1 0.8 copy-done.16
  268.9 0.8 copy-done.20
  269.6 1.0 copy-done.21
  270.7 52.8 %forward_stage.7 = (f32[128,2048]{1,0:T(8,128)}, bf16[128,2048]{1,0:T(8,128)(2,1)S(1)}, bf16[1024,256]{1,0:T(8,128)(2,1)S(1)}, bf16[8,128,2048]{2,1,0:T(8,128)(2,1)}, bf16[1024,2048]{1,0:T(8,128)(2,1)}) custom-call(bf16[4,512,128]{2,1,0:T(8,128)(2,1)S(1)} %copy-done.21, bf16[256,2048]{1,0:T(8,128)(2,1)} %copy-done.13, bf16[128,2048]{1,0:T(8,128)(2,1)} %bitcast.117, ...), custom_call_target="tpu_custom_call" | custom-call | flops 10000000000 | bytes 104857600 | tf_op jit(solution)/shard_map/forward_stage/pallas_call | solution.py:1237
  323.5 0.8 copy-done.15
  324.3 0.8 copy-done.22
  325.1 91.0 %middle_part.3 = (f32[128,2048]{1,0:T(8,128)}, bf16[128,2048]{1,0:T(8,128)(2,1)}, f32[1,2048]{1,0:T(1,128)}, bf16[4,128,2048]{2,1,0:T(8,128)(2,1)}, bf16[4,128,2...) custom-call(f32[128,2048]{1,0:T(8,128)} %get-tuple-element.95.middle, ...), custom_call_target="tpu_custom_call" | custom-call | flops 38654705664 | bytes 62914560 | tf_op jit(solution)/shard_map/middle_part/pallas_call | solution.py:1267
  416.1 97.6 %middle_part.4 = (f32[128,2048]{1,0:T(8,128)}, bf16[128,2048]{1,0:T(8,128)(2,1)}, f32[1,2048]{1,0:T(1,128)}, bf16[128,2048]{1,0:T(8,128)(2,1)}, bf16[8,128,2048]...) custom-call(f32[128,2048]{1,0:T(8,128)} %get-tuple-element.91.middle, ...), custom_call_target="tpu_custom_call" | custom-call | flops 38654705664 | bytes 62914560 | tf_op jit(solution)/shard_map/middle_part/pallas_call | solution.py:1267
  513.7 100.5 %middle_part.5 = (f32[128,2048]{1,0:T(8,128)}, bf16[128,2048]{1,0:T(8,128)(2,1)}, f32[1,2048]{1,0:T(1,128)}, bf16[128,2048]{1,0:T(8,128)(2,1)}, bf16[8,128,2048]...) custom-call(f32[128,2048]{1,0:T(8,128)} %get-tuple-element.113.middl, ...), custom_call_target="tpu_custom_call" | custom-call | flops 38654705664 | bytes 62914560 | tf_op jit(solution)/shard_map/middle_part/pallas_call | solution.py:1267
  614.3 0.0 reduce-scatter.3.cloned.1.call-update
  614.3 0.0 reduce-scatter.5.cloned.1.call-start
  614.4 0.7 reduce-scatter.5.cloned.1.call-update
  615.1 62.7 %backward_stage.4 = (bf16[1024,768]{1,0:T(8,128)(2,1)}, bf16[4,256,512]{2,1,0:T(8,128)(2,1)}, bf16[128,2048]{1,0:T(8,128)(2,1)}, bf16[8,128,2048]{2,1,0:T(8,128)(2,1)}) custom-call(bf16[1024,2048]{1,0:T(8,128)(2,1)} %bitcast.135, bf16[256,2048]{1,0:T(8,128)(2,1)} %copy-done.13, bf16[4,512,384]{2,1,0:T(8,128)(2,1)} %get-tuple-element.109.refs_2_, ...), custom_call_target="tpu_custom_call" | custom-call | flops 10000000000 | bytes 104857600 | tf_op jit(solution)/shard_map/backward_stage/pallas_call | solution.py:1362
  677.8 1.7 copy.44
  679.5 56.0 %backward_stage.5 = (f32[128,2048]{1,0:T(8,128)}, bf16[4,512,768]{2,1,0:T(8,128)(2,1)}, f32[1,2048]{1,0:T(1,128)}, bf16[1024,768]{1,0:T(8,128)(2,1)}, bf16[4,256,512]{2,1,0:T(8,128)(2,1)}) custom-call(bf16[1024,768]{1,0:T(8,128)(2,1)} %get-tuple-element.124.refs_0_, bf16[2048,768]{1,0:T(8,128)(2,1)} %copy-done.12, bf16[1024,2048]{1,0:T(8,128)(2,1)} %bitcast.102, ...), custom_call_target="tpu_custom_call" | custom-call | flops 10000000000 | bytes 104857600 | tf_op jit(solution)/shard_map/backward_stage/pallas_call | solution.py:1362
  735.5 2.0 copy.43
  737.6 1.5 dynamic_update_slice.23
  739.1 55.3 %backward_stage.6 = (f32[128,2048]{1,0:T(8,128)}, bf16[4,512,768]{2,1,0:T(8,128)(2,1)}, f32[1,2048]{1,0:T(1,128)}, bf16[1024,768]{1,0:T(8,128)(2,1)}, bf16[4,256,512]{2,1,0:T(8,128)(2,1)}) custom-call(bf16[1024,768]{1,0:T(8,128)(2,1)} %get-tuple-element.131.refs_0_, bf16[2048,768]{1,0:T(8,128)(2,1)} %copy-done.12, bf16[1024,2048]{1,0:T(8,128)(2,1)} %bitcast.133, ...), custom_call_target="tpu_custom_call" | custom-call | flops 10000000000 | bytes 104857600 | tf_op jit(solution)/shard_map/backward_stage/pallas_call | solution.py:1362
  794.4 0.7 add.40
  795.1 0.1 pad.4.clone
  795.2 0.7 maximum_maximum_fusion.refs_8_
  795.9 74.9 %backward_stage.7 = (f32[128,2048]{1,0:T(8,128)}, bf16[4,256,512]{2,1,0:T(8,128)(2,1)}, bf16[4,512,768]{2,1,0:T(8,128)(2,1)}, f32[8,2048]{1,0:T(8,128)}) custom-call(bf16[1024,768]{1,0:T(8,128)(2,1)} %get-tuple-element.139.refs_0_, bf16[2048,768]{1,0:T(8,128)(2,1)} %copy-done.12, bf16[1024,2048]{1,0:T(8,128)(2,1)} %bitcast.131, bf16[128,2048]{1,0:T(8,128)(2,1)} %bitcast.118, ...), custom_call_target="tpu_custom_call" | custom-call | flops 10000000000 | bytes 104857600 | tf_op jit(solution)/shard_map/backward_stage/pallas_call | solution.py:1362
  870.8 1.6 fusion.2
  872.4 0.6 div.16
  873.0 0.9 dynamic_update_slice.20
  873.9 2.2 convert_reduce_fusion.2
  876.2 0.4 convert_reduce_fusion.1
  876.6 1.2 fusion
  877.8 1.1 copy-done.23
  878.9 2.3 convert_reduce_fusion
  881.2 0.6 bitcast_dynamic-update-slice_fusion.3
  881.8 0.6 bitcast_dynamic-update-slice_fusion.2
  882.4 0.9 bitcast_dynamic-update-slice_fusion.1
  883.3 0.2 copy-done.26
  883.5 0.9 bitcast_dynamic-update-slice_fusion
  884.4 0.0 reduce-scatter.3.cloned.1.call-done
  884.4 3.6 convert_element_type.63
  888.0 2.8 convert_element_type.64
  (62 shorter events, 0.2 us)
Async XLA Ops:
  7.2 2.7 copy-start.32
  7.2 877.2 %reduce-scatter.3.cloned.1.call-start = ((), (), s32[]{:S(2)}) async-start(), calls=%async_computation.2 | async-start | bytes 5242880 | tf_op jit(solution)/shard_map/reduce_scatter | solution.py:1531
  9.8 9.2 %copy-start = (bf16[2,64,2048]{2,1,0:T(8,128)(2,1)}, bf16[2,64,2048]{2,1,0:T(8,128)(2,1)S(1)}, u32[]{:S(2)}) copy-start(bf16[2,64,2048]{2,1,0:T(8,128)(2,1)S(1)} %copy.25) | copy-start | bytes 1572868
  9.9 5.0 copy-start.27
  10.1 57.0 %copy-start.1 = (bf16[2,64,2048]{2,1,0:T(8,128)(2,1)}, bf16[2,64,2048]{2,1,0:T(8,128)(2,1)S(1)}, u32[]{:S(2)}) copy-start(bf16[2,64,2048]{2,1,0:T(8,128)(2,1)S(1)} %copy.26) | copy-start | bytes 1572868
  13.9 5.1 copy-start.2
  13.9 5.1 copy-start.3
  13.9 5.1 copy-start.4
  13.9 5.1 copy-start.5
  13.9 5.1 copy-start.6
  17.9 126.4 %copy-start.8 = (f32[1,1,2048]{2,1,0:T(1,128)}, f32[1,1,2048]{2,1,0:T(1,128)S(1)}, u32[]{:S(2)}) copy-start(f32[1,1,2048]{2,1,0:T(1,128)S(1)} %dynamic-slice_convert_fusion.2) | copy-start | bytes 24580
  17.9 127.1 %copy-start.10 = (f32[1,1,2048]{2,1,0:T(1,128)}, f32[1,1,2048]{2,1,0:T(1,128)S(1)}, u32[]{:S(2)}) copy-start(f32[1,1,2048]{2,1,0:T(1,128)S(1)} %get-tuple-element.174) | copy-start | bytes 24580
  17.9 190.4 %copy-start.9 = (f32[1,1,2048]{2,1,0:T(1,128)}, f32[1,1,2048]{2,1,0:T(1,128)S(1)}, u32[]{:S(2)}) copy-start(f32[1,1,2048]{2,1,0:T(1,128)S(1)} %get-tuple-element.173) | copy-start | bytes 24580
  63.3 2.1 copy-start.11
  65.4 1.7 copy-start.12
  67.1 77.2 %copy-start.13 = (bf16[256,2048]{1,0:T(8,128)(2,1)}, bf16[256,2048]{1,0:T(8,128)(2,1)S(1)}, u32[]{:S(2)}) copy-start(bf16[256,2048]{1,0:T(8,128)(2,1)S(1)} %get-tuple-element.86.refs_1_.refs_7_.refs_8_) | copy-start | bytes 3145732
  67.1 78.0 %copy-start.14 = (f32[2048]{0:T(1024)S(1)}, f32[2048]{0:T(1024)}, u32[]{:S(2)}) copy-start(f32[2048]{0:T(1024)} %param.22) | copy-start | bytes 24580
  144.3 0.8 copy-start.19
  207.6 0.8 copy-start.18
  208.4 59.7 %copy-start.17 = (bf16[1024,256]{1,0:T(8,128)(2,1)}, bf16[1024,256]{1,0:T(8,128)(2,1)S(1)}, u32[]{:S(2)}) copy-start(bf16[1024,256]{1,0:T(8,128)(2,1)S(1)} %get-tuple-element.110.refs_6_) | copy-start | bytes 1572868
  268.1 0.8 copy-start.16
  268.9 0.8 copy-start.20
  269.6 1.0 copy-start.21
  323.5 0.8 copy-start.15
  324.3 0.8 copy-start.22
  614.3 273.7 %reduce-scatter.5.cloned.1.call-start = ((), (), s32[]{:S(2)}) async-start(), calls=%async_computation.3 | async-start | bytes 5242880 | tf_op jit(solution)/shard_map/reduce_scatter | solution.py:1531
  739.0 55.3 %copy-start.33 = (f32[1,2048]{1,0:T(1,128)S(1)}, f32[1,2048]{1,0:T(1,128)}, u32[]{:S(2)}) copy-start(f32[1,2048]{1,0:T(1,128)} %get-tuple-element.146) | copy-start | bytes 24580
  739.0 56.1 %copy-start.34 = (f32[1,2048]{1,0:T(1,128)S(1)}, f32[1,2048]{1,0:T(1,128)}, u32[]{:S(2)}) copy-start(f32[1,2048]{1,0:T(1,128)} %get-tuple-element.143) | copy-start | bytes 24580
  739.1 56.1 %copy-start.35 = (f32[1,2048]{1,0:T(1,128)S(1)}, f32[1,2048]{1,0:T(1,128)}, u32[]{:S(2)}) copy-start(f32[1,2048]{1,0:T(1,128)} %get-tuple-element.144) | copy-start | bytes 24580
  739.1 56.1 %copy-start.36 = (f32[1,2048]{1,0:T(1,128)S(1)}, f32[1,2048]{1,0:T(1,128)}, u32[]{:S(2)}) copy-start(f32[1,2048]{1,0:T(1,128)} %get-tuple-element.145) | copy-start | bytes 24580
  795.9 76.5 %copy-start.7 = (f32[2048]{0:T(1024)S(1)}, f32[2048]{0:T(1024)}, u32[]{:S(2)}) copy-start(f32[2048]{0:T(1024)} %param.17) | copy-start | bytes 24580
  870.8 5.4 copy-start.25
  876.2 2.8 copy-start.23
  878.9 2.3 copy-start.30
  878.9 2.8 copy-start.31
  878.9 3.4 copy-start.28
  881.2 2.3 copy-start.29
  882.4 1.1 copy-start.26
  884.4 6.5 copy-start.24
Sparse Core Ops, SparseCore 0:
  614.4 83.7 reduce-scatter.2
  701.5 74.2 reduce-scatter.4

commit v2 on v1

--- a/solution.py
+++ b/solution.py
@@ -779,9 +779,11 @@
         pl.when(s == 2)(lambda: go_on(moving, 1))
         pl.when(s == 3)(lambda: go_on(sums[:1], 1))
 
-        @pl.loop(0, width // 256)
+        wide = math.gcd(width, 512)
+
+        @pl.loop(0, width // wide)
         def _(t):
-            cols = pl.ds(pl.multiple_of(t * 256, 256), 256)
+            cols = pl.ds(pl.multiple_of(t * wide, wide), wide)
             value = dot(act_ref[rows, :], down_ref[:, cols])
             keep, send = split_cores(spot.core, value.astype(BF16), owner_rows)
             y_mine[place, :, cols] = keep[0]

time: 907 us -> 904 us (level)
  no operation moved by 1% of the time
where the time goes in v2:
time: 904 us; the launch traced here: 895 us
  Pallas kernels  831 us (92%)
  local copies, waits for them, and re-layouts  34.5 us (4%)
  between operations  15 us (2%)
  other arithmetic  13.4 us (1%)
    pallas_call x3, Pallas kernels, middle_part(): pl.pallas_call(functools.partial(middle_kernel, not before, defer, ships,...  282 us
    pallas_call x4, Pallas kernels, forward_stage(): pl.pallas_call(functools.partial(forward_kernel, bool(tail), bool(head),...  252 us
    pallas_call x4, Pallas kernels, backward_stage(): pl.pallas_call(functools.partial(backward_kernel, bool(tail), bool(head),...  252 us
    pallas_call x1, Pallas kernels, begin(): pl.pallas_call(begin_kernel, out_shape=[shape(rows * size, 3 * columns),...  44.3 us
  transfers between devices with their start and end apart: 2, of which 0 were waited for; matrix products, arithmetic and copies ran while one was open for 3% of the time, Pallas kernels for 28%

profile of v2, /device:TPU:0, one launch (start us, length us, event | category | flops | bytes accessed | tf_op | source)
XLA Modules:
  0.0 894.9 jit_solution(11867401987060780074)
XLA Ops:
  7.2 0.0 reduce-scatter.3.cloned.1.call-start
  7.2 2.4 slice_bitcast_fusion.2
  9.7 0.2 copy.25
  9.8 0.0 copy-start
  9.9 0.2 copy.26
  10.1 0.0 copy-start.1
  10.1 2.9 slice_bitcast_fusion
  13.0 1.0 copy.27
  13.9 0.0 copy-start.6
  13.9 1.0 copy.28
  14.9 1.0 fusion.1
  15.9 1.0 copy.29
  16.9 1.0 copy.30
  17.9 0.0 copy-start.8
  17.9 0.0 copy-start.10
  17.9 1.1 constant_dynamic-slice_fusion
  19.1 44.3 %begin.1 = (bf16[2048,768]{1,0:T(8,128)(2,1)S(1)}, bf16[256,2048]{1,0:T(8,128)(2,1)S(1)}, bf16[8,128,2048]{2,1,0:T(8,128)(2,1)S(1)}) custom-call(bf16[128,2048]{1,0:T(8,128)(2,1)S(1)} %bitcast.83, f32[1,2048]{1,0:T(1,128)S(1)} %bitcast.92, bf16[512,256]{1,0:T(8,128)(2,1)S(1)} %copy-done.2, bf16[512,256]{1,0:T(8,128)(2,1)S(1)} %copy-done.3, ...), custom_call_target="tpu_custom_call" | custom-call | bytes 62914560 | tf_op jit(solution)/shard_map/begin/pallas_call | solution.py:1180
  63.4 2.0 copy-done.11
  65.4 1.7 copy-done.12
  67.1 77.2 %forward_stage.4 = (bf16[4,512,384]{2,1,0:T(8,128)(2,1)}, bf16[4,512,128]{2,1,0:T(8,128)(2,1)S(1)}, bf16[8,128,2048]{2,1,0:T(8,128)(2,1)}, bf16[8,128,2048]{2,1,0:T(8,128)(2,1)}, bf16[2048,1024]{1,0:T(8,128)(2,1)}) custom-call(bf16[1024,2048]{1,0:T(8,128)(2,1)} %bitcast.101, bf16[2048,768]{1,0:T(8,128)(2,1)} %copy-done.12, ...), custom_call_target="tpu_custom_call" | custom-call | flops 10000000000 | bytes 104857600 | tf_op jit(solution)/shard_map/forward_stage/pallas_call | solution.py:1239
  144.3 0.8 copy-done.19
  145.1 62.7 %forward_stage.5 = (f32[128,2048]{1,0:T(8,128)}, bf16[128,2048]{1,0:T(8,128)(2,1)S(1)}, bf16[1024,256]{1,0:T(8,128)(2,1)S(1)}, bf16[4,512,384]{2,1,0:T(8,128)(2,...) custom-call(bf16[4,512,128]{2,1,0:T(8,128)(2,1)} %copy-done.19, ...), custom_call_target="tpu_custom_call" | custom-call | flops 10000000000 | bytes 104857600 | tf_op jit(solution)/shard_map/forward_stage/pallas_call | solution.py:1239
  207.8 0.0 copy-start.18
  207.8 0.8 copy-done.18
  208.6 59.7 %forward_stage.6 = (f32[128,2048]{1,0:T(8,128)}, bf16[128,2048]{1,0:T(8,128)(2,1)S(1)}, bf16[1024,256]{1,0:T(8,128)(2,1)S(1)}, bf16[4,512,384]{2,1,0:T(8,128)(2,...) custom-call(bf16[4,512,128]{2,1,0:T(8,128)(2,1)} %get-tuple-element.88.refs_0_, ...), custom_call_target="tpu_custom_call" | custom-call | flops 10000000000 | bytes 104857600 | tf_op jit(solution)/shard_map/forward_stage/pallas_call | solution.py:1239
  268.3 0.8 copy-done.16
  269.1 0.8 copy-done.20
  269.9 1.0 copy-done.21
  270.9 52.8 %forward_stage.7 = (f32[128,2048]{1,0:T(8,128)}, bf16[128,2048]{1,0:T(8,128)(2,1)S(1)}, bf16[1024,256]{1,0:T(8,128)(2,1)S(1)}, bf16[8,128,2048]{2,1,0:T(8,128)(2,1)}, bf16[1024,2048]{1,0:T(8,128)(2,1)}) custom-call(bf16[4,512,128]{2,1,0:T(8,128)(2,1)S(1)} %copy-done.21, bf16[256,2048]{1,0:T(8,128)(2,1)} %copy-done.13, bf16[128,2048]{1,0:T(8,128)(2,1)} %bitcast.117, ...), custom_call_target="tpu_custom_call" | custom-call | flops 10000000000 | bytes 104857600 | tf_op jit(solution)/shard_map/forward_stage/pallas_call | solution.py:1239
  323.7 0.8 copy-done.15
  324.5 0.8 copy-done.22
  325.3 89.4 %middle_part.3 = (f32[128,2048]{1,0:T(8,128)}, bf16[128,2048]{1,0:T(8,128)(2,1)}, f32[1,2048]{1,0:T(1,128)}, bf16[4,128,2048]{2,1,0:T(8,128)(2,1)}, bf16[4,128,2...) custom-call(f32[128,2048]{1,0:T(8,128)} %get-tuple-element.95.middle, ...), custom_call_target="tpu_custom_call" | custom-call | flops 38654705664 | bytes 62914560 | tf_op jit(solution)/shard_map/middle_part/pallas_call | solution.py:1269
  414.7 95.7 %middle_part.4 = (f32[128,2048]{1,0:T(8,128)}, bf16[128,2048]{1,0:T(8,128)(2,1)}, f32[1,2048]{1,0:T(1,128)}, bf16[128,2048]{1,0:T(8,128)(2,1)}, bf16[8,128,2048]...) custom-call(f32[128,2048]{1,0:T(8,128)} %get-tuple-element.91.middle, ...), custom_call_target="tpu_custom_call" | custom-call | flops 38654705664 | bytes 62914560 | tf_op jit(solution)/shard_map/middle_part/pallas_call | solution.py:1269
  510.4 97.3 %middle_part.5 = (f32[128,2048]{1,0:T(8,128)}, bf16[128,2048]{1,0:T(8,128)(2,1)}, f32[1,2048]{1,0:T(1,128)}, bf16[128,2048]{1,0:T(8,128)(2,1)}, bf16[8,128,2048]...) custom-call(f32[128,2048]{1,0:T(8,128)} %get-tuple-element.113.middl, ...), custom_call_target="tpu_custom_call" | custom-call | flops 38654705664 | bytes 62914560 | tf_op jit(solution)/shard_map/middle_part/pallas_call | solution.py:1269
  607.7 0.0 reduce-scatter.3.cloned.1.call-update
  607.8 0.0 reduce-scatter.5.cloned.1.call-start
  607.8 0.7 reduce-scatter.5.cloned.1.call-update
  608.5 65.1 %backward_stage.4 = (bf16[1024,768]{1,0:T(8,128)(2,1)}, bf16[4,256,512]{2,1,0:T(8,128)(2,1)}, bf16[128,2048]{1,0:T(8,128)(2,1)}, bf16[8,128,2048]{2,1,0:T(8,128)(2,1)}) custom-call(bf16[1024,2048]{1,0:T(8,128)(2,1)} %bitcast.135, bf16[256,2048]{1,0:T(8,128)(2,1)} %copy-done.13, bf16[4,512,384]{2,1,0:T(8,128)(2,1)} %get-tuple-element.109.refs_2_, ...), custom_call_target="tpu_custom_call" | custom-call | flops 10000000000 | bytes 104857600 | tf_op jit(solution)/shard_map/backward_stage/pallas_call | solution.py:1364
  673.6 1.7 copy.44
  675.3 56.6 %backward_stage.5 = (f32[128,2048]{1,0:T(8,128)}, bf16[4,512,768]{2,1,0:T(8,128)(2,1)}, f32[1,2048]{1,0:T(1,128)}, bf16[1024,768]{1,0:T(8,128)(2,1)}, bf16[4,256,512]{2,1,0:T(8,128)(2,1)}) custom-call(bf16[1024,768]{1,0:T(8,128)(2,1)} %get-tuple-element.124.refs_0_, bf16[2048,768]{1,0:T(8,128)(2,1)} %copy-done.12, bf16[1024,2048]{1,0:T(8,128)(2,1)} %bitcast.102, ...), custom_call_target="tpu_custom_call" | custom-call | flops 10000000000 | bytes 104857600 | tf_op jit(solution)/shard_map/backward_stage/pallas_call | solution.py:1364
  731.9 2.0 copy.43
  733.9 1.5 dynamic_update_slice.23
  735.4 55.1 %backward_stage.6 = (f32[128,2048]{1,0:T(8,128)}, bf16[4,512,768]{2,1,0:T(8,128)(2,1)}, f32[1,2048]{1,0:T(1,128)}, bf16[1024,768]{1,0:T(8,128)(2,1)}, bf16[4,256,512]{2,1,0:T(8,128)(2,1)}) custom-call(bf16[1024,768]{1,0:T(8,128)(2,1)} %get-tuple-element.131.refs_0_, bf16[2048,768]{1,0:T(8,128)(2,1)} %copy-done.12, bf16[1024,2048]{1,0:T(8,128)(2,1)} %bitcast.133, ...), custom_call_target="tpu_custom_call" | custom-call | flops 10000000000 | bytes 104857600 | tf_op jit(solution)/shard_map/backward_stage/pallas_call | solution.py:1364
  790.5 0.7 add.40
  791.2 0.1 pad.4.clone
  791.3 0.7 maximum_maximum_fusion.refs_8_
  792.0 75.5 %backward_stage.7 = (f32[128,2048]{1,0:T(8,128)}, bf16[4,256,512]{2,1,0:T(8,128)(2,1)}, bf16[4,512,768]{2,1,0:T(8,128)(2,1)}, f32[8,2048]{1,0:T(8,128)}) custom-call(bf16[1024,768]{1,0:T(8,128)(2,1)} %get-tuple-element.139.refs_0_, bf16[2048,768]{1,0:T(8,128)(2,1)} %copy-done.12, bf16[1024,2048]{1,0:T(8,128)(2,1)} %bitcast.131, bf16[128,2048]{1,0:T(8,128)(2,1)} %bitcast.118, ...), custom_call_target="tpu_custom_call" | custom-call | flops 10000000000 | bytes 104857600 | tf_op jit(solution)/shard_map/backward_stage/pallas_call | solution.py:1364
  867.6 1.6 fusion.2
  869.2 0.6 div.16
  869.8 0.9 dynamic_update_slice.20
  870.7 2.2 convert_reduce_fusion.2
  873.0 0.4 convert_reduce_fusion.1
  873.4 1.2 fusion
  874.6 1.1 copy-done.23
  875.7 2.3 convert_reduce_fusion
  878.0 0.6 bitcast_dynamic-update-slice_fusion.3
  878.6 0.6 bitcast_dynamic-update-slice_fusion.2
  879.1 0.0 copy-start.26
  879.2 0.9 bitcast_dynamic-update-slice_fusion.1
  880.1 0.2 copy-done.26
  880.3 0.9 bitcast_dynamic-update-slice_fusion
  881.2 0.0 reduce-scatter.3.cloned.1.call-done
  881.2 3.6 convert_element_type.63
  884.8 2.8 convert_element_type.64
  (62 shorter events, 0.2 us)
Async XLA Ops:
  7.2 2.7 copy-start.32
  7.2 874.0 %reduce-scatter.3.cloned.1.call-start = ((), (), s32[]{:S(2)}) async-start(), calls=%async_computation.2 | async-start | bytes 5242880 | tf_op jit(solution)/shard_map/reduce_scatter | solution.py:1533
  9.8 9.2 %copy-start = (bf16[2,64,2048]{2,1,0:T(8,128)(2,1)}, bf16[2,64,2048]{2,1,0:T(8,128)(2,1)S(1)}, u32[]{:S(2)}) copy-start(bf16[2,64,2048]{2,1,0:T(8,128)(2,1)S(1)} %copy.25) | copy-start | bytes 1572868
  9.9 5.0 copy-start.27
  10.1 57.0 %copy-start.1 = (bf16[2,64,2048]{2,1,0:T(8,128)(2,1)}, bf16[2,64,2048]{2,1,0:T(8,128)(2,1)S(1)}, u32[]{:S(2)}) copy-start(bf16[2,64,2048]{2,1,0:T(8,128)(2,1)S(1)} %copy.26) | copy-start | bytes 1572868
  13.9 5.1 copy-start.2
  13.9 5.1 copy-start.3
  13.9 5.1 copy-start.4
  13.9 5.1 copy-start.5
  13.9 5.1 copy-start.6
  17.9 126.4 %copy-start.8 = (f32[1,1,2048]{2,1,0:T(1,128)}, f32[1,1,2048]{2,1,0:T(1,128)S(1)}, u32[]{:S(2)}) copy-start(f32[1,1,2048]{2,1,0:T(1,128)S(1)} %dynamic-slice_convert_fusion.2) | copy-start | bytes 24580
  17.9 127.1 %copy-start.10 = (f32[1,1,2048]{2,1,0:T(1,128)}, f32[1,1,2048]{2,1,0:T(1,128)S(1)}, u32[]{:S(2)}) copy-start(f32[1,1,2048]{2,1,0:T(1,128)S(1)} %get-tuple-element.174) | copy-start | bytes 24580
  17.9 190.6 %copy-start.9 = (f32[1,1,2048]{2,1,0:T(1,128)}, f32[1,1,2048]{2,1,0:T(1,128)S(1)}, u32[]{:S(2)}) copy-start(f32[1,1,2048]{2,1,0:T(1,128)S(1)} %get-tuple-element.173) | copy-start | bytes 24580
  63.3 2.1 copy-start.11
  65.4 1.7 copy-start.12
  67.1 77.2 %copy-start.13 = (bf16[256,2048]{1,0:T(8,128)(2,1)}, bf16[256,2048]{1,0:T(8,128)(2,1)S(1)}, u32[]{:S(2)}) copy-start(bf16[256,2048]{1,0:T(8,128)(2,1)S(1)} %get-tuple-element.86.refs_1_.refs_7_.refs_8_) | copy-start | bytes 3145732
  67.1 78.0 %copy-start.14 = (f32[2048]{0:T(1024)S(1)}, f32[2048]{0:T(1024)}, u32[]{:S(2)}) copy-start(f32[2048]{0:T(1024)} %param.22) | copy-start | bytes 24580
  144.3 0.8 copy-start.19
  207.8 0.8 copy-start.18
  208.6 59.7 %copy-start.17 = (bf16[1024,256]{1,0:T(8,128)(2,1)}, bf16[1024,256]{1,0:T(8,128)(2,1)S(1)}, u32[]{:S(2)}) copy-start(bf16[1024,256]{1,0:T(8,128)(2,1)S(1)} %get-tuple-element.110.refs_6_) | copy-start | bytes 1572868
  268.3 0.8 copy-start.16
  269.1 0.8 copy-start.20
  269.8 1.0 copy-start.21
  323.7 0.8 copy-start.15
  324.5 0.8 copy-start.22
  607.8 277.0 %reduce-scatter.5.cloned.1.call-start = ((), (), s32[]{:S(2)}) async-start(), calls=%async_computation.3 | async-start | bytes 5242880 | tf_op jit(solution)/shard_map/reduce_scatter | solution.py:1533
  735.4 55.1 %copy-start.33 = (f32[1,2048]{1,0:T(1,128)S(1)}, f32[1,2048]{1,0:T(1,128)}, u32[]{:S(2)}) copy-start(f32[1,2048]{1,0:T(1,128)} %get-tuple-element.146) | copy-start | bytes 24580
  735.4 55.9 %copy-start.34 = (f32[1,2048]{1,0:T(1,128)S(1)}, f32[1,2048]{1,0:T(1,128)}, u32[]{:S(2)}) copy-start(f32[1,2048]{1,0:T(1,128)} %get-tuple-element.143) | copy-start | bytes 24580
  735.4 55.9 %copy-start.35 = (f32[1,2048]{1,0:T(1,128)S(1)}, f32[1,2048]{1,0:T(1,128)}, u32[]{:S(2)}) copy-start(f32[1,2048]{1,0:T(1,128)} %get-tuple-element.144) | copy-start | bytes 24580
  735.4 55.9 %copy-start.36 = (f32[1,2048]{1,0:T(1,128)S(1)}, f32[1,2048]{1,0:T(1,128)}, u32[]{:S(2)}) copy-start(f32[1,2048]{1,0:T(1,128)} %get-tuple-element.145) | copy-start | bytes 24580
  792.0 77.2 %copy-start.7 = (f32[2048]{0:T(1024)S(1)}, f32[2048]{0:T(1024)}, u32[]{:S(2)}) copy-start(f32[2048]{0:T(1024)} %param.17) | copy-start | bytes 24580
  867.5 5.4 copy-start.25
  873.0 2.8 copy-start.23
  875.7 2.3 copy-start.30
  875.7 2.8 copy-start.31
  875.7 3.4 copy-start.28
  878.0 2.3 copy-start.29
  879.1 1.1 copy-start.26
  881.2 6.5 copy-start.24
Sparse Core Ops, SparseCore 0:
  607.9 86.7 reduce-scatter.2
  697.9 74.9 reduce-scatter.4
